TPU v7x, 32 devices: a whole 2x2x4 slice. The times are simulated.
32 devices in a mesh: groups: 2 (over x), dev: 8 (over z, y), rve: 2 (over core).
Axes of the slice: x: 2, y: 2, z: 4, core: 2. Of those that a mesh axis runs over, the one named last changes fastest.
Arguments:
- phase: int32 [4, 64, 128, 128], P(('groups', 'rve'), 'dev'), parts along dimension 0, may hold values from 0 to 2
- load_case: int32 [4], P(('groups', 'rve')), parts along dimension 0, may hold values from 0 to 5
- moduli: float32 [2, 3], replicated, may hold values from 0.5 to 8
- loading_table: float32 [6, 3, 3], replicated, may hold values from -4 to 4
- w_embed: bfloat16 [1408, 768], P(('dev', 'rve')), may hold values from -0.21875 to 0.21875
- w_up: bfloat16 [3072, 1408], P(('dev', 'rve')), may hold values from -0.15625 to 0.15625
- cotangent: bfloat16 [16384, 3072], P(('groups', 'dev', 'rve')), parts along dimension 0, may hold values from -6 to 6
Outputs:
- displacement: float32 [4, 3, 64, 128, 128], P(('groups', 'rve'), None, 'dev'), parts along dimension 0
- grad_embed: float32 [2816, 768], P(('groups', 'dev', 'rve')), parts along dimension 0
- grad_up: float32 [6144, 1408], P(('groups', 'dev', 'rve')), parts along dimension 0
There are 2 independent parts, one for each index of `groups`. A program takes and returns all parts, laid end to end along the dimension named above; an argument that names none is the same for every part. Nothing has to cross between parts.
Inputs may be any that keep to these rules, and one draw needn't show every extreme that they name: `load_case`: row of loading_table for each RVE.
All inputs are finite; a program needn't handle non-finite values.
Results may differ from a plain program's by a relative error of at most 0.0069.
Values may be sent and summed in bfloat16 or wider, within the bound.
A program may use at most 128 MiB of HBM per device.

v0:
```python
from functools import partial
import math

import jax
import jax.numpy as jnp
from jax import lax
from jax.sharding import PartitionSpec as P

PATCH_X = 8
PATCH_Y = 8
PATCH_Z = 4
SWEEPS = 4


epsilon = 1e-06


def with_halo(value, sides, width):
    for axis, dim in sides:
        size, length = (lax.axis_size(axis), value.shape[dim])
        up = [(i, (i + 1) % size) for i in range(size - 1)]
        down = [(j, i) for i, j in up]
        last = lax.slice_in_dim(value, length - width, length, axis=dim)
        initial = lax.slice_in_dim(value, 0, width, axis=dim)
        before = lax.ppermute(last, axis, up)
        after = lax.ppermute(initial, axis, down)
        value = jnp.concatenate([before, value, after], axis=dim)
    return value


def stiffness(phase, moduli):
    labels = jnp.arange(moduli.shape[1], dtype=jnp.int32)
    member = (labels[:, None, None, None] == phase[None]).astype(jnp.float32)
    shear_stiff = jnp.sum(member * moduli[0][:, None, None, None], axis=0)
    axial_stiff = jnp.sum(member * moduli[1][:, None, None, None], axis=0)
    return (shear_stiff, axial_stiff)


def harmonic(here, there, in_here, in_there):
    blended = 2.0 * here * there / (here + there)
    return jnp.where(in_here & in_there, blended, jnp.where(in_here, here, there))


def face_pairs(stiff, inside):
    stiff = jnp.where(inside, stiff, 1.0)
    padded = jnp.pad(stiff, 1, constant_values=1.0)
    in_pad = jnp.pad(inside, 1)
    face_list = []
    for direction in range(3):
        upper_cut = [slice(1, -1)] * 3
        lower_cut = [slice(1, -1)] * 3
        upper_cut[direction] = slice(2, None)
        lower_cut[direction] = slice(0, -2)
        upper_face = harmonic(stiff, padded[tuple(upper_cut)], inside, in_pad[tuple(upper_cut)])
        lower_face = harmonic(stiff, padded[tuple(lower_cut)], inside, in_pad[tuple(lower_cut)])
        face_list.append((upper_face, lower_face))
    return face_list


def operator_terms(shear_stiff, axial_stiff, inside, strain):
    shear_faces = face_pairs(shear_stiff, inside)
    axial_faces = face_pairs(axial_stiff, inside)
    terms = []
    for component in range(3):
        face_list = [
            axial_faces[direction] if direction == component else shear_faces[direction]
            for direction in range(3)
        ]
        forcing = strain[component, 0] * (face_list[0][0] - face_list[0][1])
        diagonal = face_list[0][0] + face_list[0][1]
        for direction in (1, 2):
            forcing = forcing + strain[component, direction] * (
                face_list[direction][0] - face_list[direction][1]
            )
            diagonal = diagonal + face_list[direction][0] + face_list[direction][1]
        terms.append((face_list, forcing, diagonal))
    return terms


def first_iterate(terms, inside):
    return jnp.stack(
        [jnp.where(inside, forcing / diagonal, 0.0) for face_list, forcing, diagonal in terms]
    )


def jacobi_sweep(ghosted, terms, inside):
    results = []
    for component in range(3):
        face_list, forcing, diagonal = terms[component]
        padded = jnp.pad(ghosted[component], ((0, 0), (1, 1), (1, 1)))
        summed = forcing
        for direction in range(3):
            upper_cut = [slice(1, -1)] * 3
            lower_cut = [slice(1, -1)] * 3
            upper_cut[direction] = slice(2, None)
            lower_cut[direction] = slice(0, -2)
            summed = (
                summed
                + face_list[direction][0] * padded[tuple(upper_cut)]
                + face_list[direction][1] * padded[tuple(lower_cut)]
            )
        results.append(jnp.where(inside, summed / diagonal, 0.0))
    return jnp.stack(results)


def row_mask(first_global, row_total, grid_rows, plane_shape):
    global_rows = first_global + jnp.arange(row_total, dtype=jnp.int32)
    within = (global_rows >= 0) & (global_rows < grid_rows)
    return jnp.broadcast_to(within[:, None, None], (row_total,) + tuple(plane_shape))


def contract_last(left, right):
    return lax.dot_general(
        left, right, (((1,), (1,)), ((), ())), preferred_element_type=jnp.float32
    )


def contract_first(left, right):
    return lax.dot_general(
        left, right, (((0,), (0,)), ((), ())), preferred_element_type=jnp.float32
    )


def gelu_grad(pre_act, cotangent):
    _, pullback = jax.vjp(partial(jax.nn.gelu, approximate=True), pre_act)
    return pullback(cotangent.astype(jnp.float32))[0].astype(jnp.bfloat16)


def local(phase, load_case, moduli, loading_table, w_embed, w_up, cotangent):
    local_phase = phase[0]
    slab_rows = local_phase.shape[0]
    plane_shape = local_phase.shape[1:]
    dev_count = lax.axis_size("dev")
    rve_count = lax.axis_size("rve")
    first_row = lax.axis_index("dev") * slab_rows
    grid_rows = slab_rows * dev_count
    shear_stiff, axial_stiff = stiffness(local_phase, moduli)
    case_labels = jnp.arange(loading_table.shape[0], dtype=jnp.int32)
    case_pick = (case_labels == load_case[0]).astype(jnp.float32)
    strain = jnp.sum(case_pick[:, None, None] * loading_table, axis=0)
    stacked = jnp.stack([shear_stiff, axial_stiff])
    ghosted = with_halo(stacked, (("dev", 1),), SWEEPS)
    inside = row_mask(first_row - SWEEPS, slab_rows + 2 * SWEEPS, grid_rows, plane_shape)
    terms = operator_terms(ghosted[0], ghosted[1], inside, strain)
    displace = first_iterate(terms, inside)
    for repeat in range(SWEEPS - 1):
        displace = jacobi_sweep(jnp.pad(displace, ((0, 0), (1, 1), (0, 0), (0, 0))), terms, inside)
    displace = displace[:, SWEEPS : SWEEPS + slab_rows]
    rounded = displace.astype(jnp.bfloat16)
    ny_cells = rounded.shape[2]
    nz_cells = rounded.shape[3]
    band_rows = ny_cells // dev_count
    blocks = rounded.reshape(3, slab_rows, dev_count, band_rows, nz_cells)
    regrouped = lax.all_to_all(blocks, "dev", split_axis=2, concat_axis=1, tiled=True)
    grid_x = regrouped.shape[1]
    cells = regrouped.reshape(
        3, grid_x // PATCH_X, PATCH_X, band_rows // PATCH_Y, PATCH_Y, nz_cells // PATCH_Z, PATCH_Z
    )
    patches = cells.transpose(3, 1, 5, 0, 2, 4, 6).reshape(-1, 3 * PATCH_X * PATCH_Y * PATCH_Z)
    token_count = patches.shape[0]
    grad_scale = 1.0 / math.sqrt(token_count * dev_count * rve_count)
    embedded = contract_last(
        patches, lax.all_gather(w_embed, ("dev", "rve"), axis=0, tiled=True)
    ).astype(jnp.bfloat16)
    embed_wide = embedded.astype(jnp.float32)
    inverse_rms = lax.rsqrt(jnp.mean(embed_wide * embed_wide, axis=-1, keepdims=True) + epsilon)
    normed_wide = embed_wide * inverse_rms
    normed = normed_wide.astype(jnp.bfloat16)
    up_all = lax.all_gather(w_up, ("dev", "rve"), axis=0, tiled=True)
    pre_act = contract_last(normed, up_all)
    act_grad = gelu_grad(pre_act, cotangent)
    columns = act_grad
    grad_up = (
        lax.psum_scatter(
            contract_first(columns, normed), ("dev", "rve"), scatter_dimension=0, tiled=True
        )
        * grad_scale
    )
    normed_grad = jnp.dot(act_grad, up_all, preferred_element_type=jnp.float32)
    embed_in_grad = (
        inverse_rms
        * (normed_grad - normed_wide * jnp.mean(normed_grad * normed_wide, axis=-1, keepdims=True))
    ).astype(jnp.bfloat16)
    columns = embed_in_grad
    grad_embed = (
        lax.psum_scatter(
            contract_first(columns, patches), ("dev", "rve"), scatter_dimension=0, tiled=True
        )
        * grad_scale
    )
    return (displace[None], grad_embed, grad_up)


def solution(mesh):
    return jax.shard_map(
        local,
        mesh=mesh,
        in_specs=(
            P(("groups", "rve"), "dev", None, None),
            P(("groups", "rve")),
            P(),
            P(),
            P(("dev", "rve"), None),
            P(("dev", "rve"), None),
            P(("groups", "dev", "rve"), None),
        ),
        out_specs=(
            P(("groups", "rve"), None, "dev", None, None),
            P(("groups", "dev", "rve"), None),
            P(("groups", "dev", "rve"), None),
        ),
        check_vma=False,
    )
```

profile of v0, /device:TPU:0, one launch (start us, length us, event | category | flops | bytes accessed | tf_op | source)
XLA Modules:
  0.0 484.2 jit_solution(5209808814416989539)
XLA Ops:
  12.4 5.5 %collective-permute-start = (f32[2,4,128,128]{3,2,1,0:T(8,128)S(1)}, f32[2,4,128,128]{3,2,1,0:T(8,128)S(1)}, u32[]{:S(2)}, u32[]{:S(2)}) collective-permute-start(f32[2,4,128,128]{3,2,1,0:T(8,128)S(1)} %get-tuple-element.31), channel_id=1, source_target_pairs={{0,2},{2,4},{4,6},{6,8},{8,10},{10,12},{12,14},{1,3},{3,5},{5,7},{... | collective-permute-start | bytes 1572872 | tf_op jit(solution)/shard_map/ppermute | solution.py:25
  19.3 10.0 %collective-permute-done.1 = f32[2,4,128,128]{3,2,1,0:T(8,128)S(1)} collective-permute-done((f32[2,4,128,128]{3,2,1,0:T(8,128)S(1)}, f32[2,4,128,128]{3,2,1,0:T(8,128)S(1)}, u32[]{:S(2)}, u32[]{:S(2)}) %collective-permute-start.1) | collective-permute-done | bytes 524320 | tf_op jit(solution)/shard_map/ppermute | solution.py:26
  29.3 11.4 %collective-permute-done = f32[2,4,128,128]{3,2,1,0:T(8,128)S(1)} collective-permute-done((f32[2,4,128,128]{3,2,1,0:T(8,128)S(1)}, f32[2,4,128,128]{3,2,1,0:T(8,128)S(1)}, u32[]{:S(2)}, u32[]{:S(2)}) %collective-permute-start) | collective-permute-done | bytes 524320 | tf_op jit(solution)/shard_map/ppermute | solution.py:25
  41.2 5.2 %select_bitcast_fusion.11 = (f32[1,16,128,128]{3,2,1,0:T(8,128)S(1)}, f32[16,128,128]{2,1,0:T(8,128)S(1)}, f32[16,128,128]{2,1,0:T(8,128)S(1)}, f32[16,128,128]{...) fusion(f32[]{:T(128)} %bitcast.10, f32[]{:T(128)} %bitcast.8, ...), kind=kLoop, calls=%fused_computation.274 | loop fusion | flops 13893632 | bytes 9699356 | tf_op jit(solution)/shard_map/stack | solution.py:81
  46.4 4.3 select_bitcast_fusion.10
  50.7 3.5 select_bitcast_fusion.9
  55.1 3.5 select_bitcast_fusion.6
  61.9 3.3 select_bitcast_fusion.8
  66.1 3.5 select_bitcast_fusion.3
  72.9 3.3 select_bitcast_fusion.5
  77.1 3.5 select_bitcast_fusion
  83.9 3.3 select_bitcast_fusion.2
  87.6 42.6 %all_to_all.15 = bf16[3,8,8,16,128]{4,3,1,0,2:T(8,128)(2,1)S(1)} all-to-all(bf16[3,8,8,16,128]{4,3,1,0,2:T(8,128)(2,1)S(1)} %copy.17), channel_id=1, replica_groups=mesh['groups'=2,'dev'=8,'rve'=2] {'dev'}, dimensions={2} | all-to-all | bytes 1572864 | tf_op jit(solution)/shard_map/all_to_all | solution.py:154
  130.2 4.5 copy.18
  134.8 21.6 %reshape.61 = bf16[3,8,8,2,8,32,4]{4,3,6,5,2,1,0:T(2,128)(2,1)} reshape(bf16[3,8,8,1,16,128]{4,5,2,1,0,3:T(8,128)(2,1)} %copy.18) | data formatting | bytes 1572864 | tf_op jit(solution)/shard_map/reshape | solution.py:156
  156.4 29.5 %copy.19 = bf16[2,8,32,3,8,8,4]{2,1,0,6,5,4,3:T(8,128)(2,1)S(1)} copy(bf16[2,8,32,3,8,8,4]{5,0,6,2,4,1,3:T(2,128)(2,1)} %bitcast.270) | data formatting | bytes 1572864 | tf_op jit(solution)/shard_map/transpose | solution.py:159
  185.9 3.8 reshape.62
  189.7 3.4 fusion.18
  193.1 12.2 %fusion.2 = bf16[512,3072]{1,0:T(8,128)(2,1)S(1)} fusion(bf16[512,3072]{1,0:T(8,128)(2,1)} %param.13, bf16[3072,1408]{1,0:T(8,128)(2,1)} %all-gather.5.cloned.1.call-done, bf16[512,1408]{1,0:T(8,128)(2,1)S(1)} %get-tuple-element.45, f32[512]{0:T(512)S(1)} %add_rsqrt_fusion), kind=kOutput, calls=%fused_computation.6 | convolution fusion | flops 4464377856 | bytes 16386048 | tf_op jit(solution)/shard_map/dot_general | solution.py:113
  205.4 5.1 %fusion.14 = (f32[512]{0:T(512)S(1)}, f32[512,1408]{1,0:T(8,128)S(1)}) fusion(bf16[512,1408]{1,0:T(8,128)(2,1)S(1)} %get-tuple-element.45, f32[512]{0:T(512)S(1)} %add_rsqrt_fusion, bf16[512,3072]{1,0:T(8,128)(2,1)S(1)} %fusion.2, bf16[3072,1408]{1,0:T(8,128)(2,1)S(1)} %copy-done.8), kind=kOutput, calls=%fused_computation.83 | convolution fusion | flops 4432068096 | bytes 16125952 | tf_op jit(solution)/shard_map/dot_general | solution.py:179
  210.5 3.7 fusion.19
  214.3 11.0 %fusion.150 = f32[3072,1408]{1,0:T(8,128)} fusion(bf16[512,3072]{1,0:T(8,128)(2,1)} %copy-done.9, bf16[512,1408]{1,0:T(8,128)(2,1)S(1)} %get-tuple-element.45, f32[512]{0:T(512)S(1)} %add_rsqrt_fusion), kind=kOutput, calls=%fused_computation.289 | convolution fusion | flops 4431347712 | bytes 21891072 | tf_op jit(solution)/shard_map/dot_general | solution.py:119
  228.5 59.8 %reduce-scatter.3.cloned.1.call-done = f32[88,768]{1,0:T(8,128)} async-done(((f32[1408,768]{1,0:T(8,128)}), f32[88,768]{1,0:T(8,128)}) %reduce-scatter.3.cloned.1.call-update) | async-done | bytes 270352 | tf_op jit(solution)/shard_map/reduce_scatter | solution.py:186
  290.0 185.4 %reduce-scatter.5.cloned.1.call-done = f32[192,1408]{1,0:T(8,128)} async-done(((f32[3072,1408]{1,0:T(8,128)}), f32[192,1408]{1,0:T(8,128)}) %reduce-scatter.5.cloned.1.call-update) | async-done | bytes 1081360 | tf_op jit(solution)/shard_map/reduce_scatter | solution.py:174
  (57 shorter events, 26.6 us)
Async XLA Ops:
  7.2 11.4 %copy-start.7 = (f32[6,3,3]{0,2,1:T(4,128)S(1)}, f32[6,3,3]{0,2,1:T(4,128)}, u32[]{:S(2)}) copy-start(f32[6,3,3]{0,2,1:T(4,128)} %param.10) | copy-start | bytes 652
  7.2 182.5 %all-gather.3.cloned.1.call-start = ((), (), s32[]{:S(2)}) async-start(), calls=%async_computation.3 | async-start | bytes 2297856 | tf_op jit(solution)/shard_map/all_gather | solution.py:163
  7.9 185.2 %all-gather.5.cloned.1.call-start = ((), (), s32[]{:S(2)}) async-start(), calls=%async_computation.4 | async-start | bytes 9191424 | tf_op jit(solution)/shard_map/all_gather | solution.py:169
  8.7 279.6 %reduce-scatter.3.cloned.1.call-start = ((), (), s32[]{:S(2)}) async-start(), calls=%async_computation.5 | async-start | bytes 4595712 | tf_op jit(solution)/shard_map/reduce_scatter | solution.py:186
  11.1 18.2 %collective-permute-start.1 = (f32[2,4,128,128]{3,2,1,0:T(8,128)S(1)}, f32[2,4,128,128]{3,2,1,0:T(8,128)S(1)}, u32[]{:S(2)}, u32[]{:S(2)}) collective-permute-start(f32[2,4,128,128]{3,2,1,0:T(8,128)S(1)} %get-tuple-element.32), channel_id=1, source_target_pairs={{2,0},{4,2},{6,4},{8,6},{10,8},{12,10},{14,12},{3,1},{5,3},{7,5},{... | collective-permute-start | bytes 1572872 | tf_op jit(solution)/shard_map/ppermute | solution.py:26
  12.4 28.3 %collective-permute-start = (f32[2,4,128,128]{3,2,1,0:T(8,128)S(1)}, f32[2,4,128,128]{3,2,1,0:T(8,128)S(1)}, u32[]{:S(2)}, u32[]{:S(2)}) collective-permute-start(f32[2,4,128,128]{3,2,1,0:T(8,128)S(1)} %get-tuple-element.31), channel_id=1, source_target_pairs={{0,2},{2,4},{4,6},{6,8},{8,10},{10,12},{12,14},{1,3},{3,5},{5,7},{... | collective-permute-start | bytes 1572872 | tf_op jit(solution)/shard_map/ppermute | solution.py:25
  80.6 6.7 %copy-start = (f32[1,16,128,128]{3,2,1,0:T(8,128)}, f32[1,16,128,128]{3,2,1,0:T(8,128)S(1)}, u32[]{:S(2)}) copy-start(f32[1,16,128,128]{3,2,1,0:T(8,128)S(1)} %select_bitcast_fusion) | copy-start | bytes 3145732
  83.9 3.4 copy-start.2
  87.2 43.0 %copy-start.4 = (f32[1,16,128,128]{3,2,1,0:T(8,128)}, f32[1,16,128,128]{3,2,1,0:T(8,128)S(1)}, u32[]{:S(2)}) copy-start(f32[1,16,128,128]{3,2,1,0:T(8,128)S(1)} %select_bitcast_fusion.2) | copy-start | bytes 3145732
  193.1 12.2 %copy-start.8 = (bf16[3072,1408]{1,0:T(8,128)(2,1)S(1)}, bf16[3072,1408]{1,0:T(8,128)(2,1)}, u32[]{:S(2)}) copy-start(bf16[3072,1408]{1,0:T(8,128)(2,1)} %all-gather.5.cloned.1.call-done) | copy-start | bytes 25952260
  205.3 5.1 %copy-start.9 = (bf16[512,3072]{1,0:T(8,128)(2,1)}, bf16[512,3072]{1,0:T(8,128)(2,1)S(1)}, u32[]{:S(2)}) copy-start(bf16[512,3072]{1,0:T(8,128)(2,1)S(1)} %fusion.2) | copy-start | bytes 9437188
  205.3 5.1 %copy-start.6 = (bf16[512,768]{0,1:T(8,128)(2,1)S(1)}, bf16[512,768]{0,1:T(8,128)(2,1)}, u32[]{:S(2)}) copy-start(bf16[512,768]{0,1:T(8,128)(2,1)} %reshape.62) | copy-start | bytes 2359300
  214.2 261.1 %reduce-scatter.5.cloned.1.call-start = ((), (), s32[]{:S(2)}) async-start(), calls=%async_computation.6 | async-start | bytes 18382848 | tf_op jit(solution)/shard_map/reduce_scatter | solution.py:174
  225.2 1.3 copy-start.1
  225.3 1.7 copy-start.3
  225.3 2.0 copy-start.5
Sparse Core Ops, SparseCore 0:
  10.3 54.3 all-gather.2
  66.9 83.3 all-gather.4
  214.3 73.9 reduce-scatter.2
  292.3 182.9 reduce-scatter.4
where the time goes:
time: 486 us; the launch traced here: 484 us
  waiting for transfers between devices  268 us (55%)
  local copies, waits for them, and re-layouts  64.5 us (13%)
  other arithmetic  52.1 us (11%)
  blocking collectives  42.6 us (9%)
  matrix products  35.4 us (7%)
  between operations  14.8 us (3%)
  starting transfers between devices  6.98 us (1%)
    reduce_scatter x1, waiting for transfers between devices, local(): lax.psum_scatter(contract_first(columns, normed), ('dev', 'rve'), scatter...  185 us
    reduce_scatter x1, waiting for transfers between devices, local(): lax.psum_scatter(contract_first(columns, patches), ('dev', 'rve'), scatte...  59.8 us
    all_to_all x1, blocking collectives, local(): lax.all_to_all(blocks, 'dev', split_axis=2, concat_axis=1, tiled=True)  42.6 us
    another operation x11, other arithmetic, jacobi_sweep(): return jnp.stack(results)  31.2 us
    transpose x1, local copies, waits for them, and re-layouts, local(): cells.transpose(3, 1, 5, 0, 2, 4, 6)  29.5 us
    reshape x1, local copies, waits for them, and re-layouts, local(): regrouped.reshape(3, grid_x // PATCH_X, PATCH_X, band_rows // PATCH_Y, PA...  21.6 us
    dot_general x2, matrix products, contract_last(): lax.dot_general(left, right, (((1,), (1,)), ((), ())), preferred_element_...  15.6 us
    dot_general x2, matrix products, contract_first(): lax.dot_general(left, right, (((0,), (0,)), ((), ())), preferred_element_...  14.7 us
  transfers between devices with their start and end apart: 6, of which 4 were waited for; matrix products, arithmetic and copies ran while one was open for 26% of the time, Pallas kernels for 0%

commit v1 on v0

--- a/solution.py
+++ b/solution.py
@@ -4,6 +4,8 @@
 import jax
 import jax.numpy as jnp
 from jax import lax
+from jax.experimental import pallas as pl
+from jax.experimental.pallas import tpu as pltpu
 from jax.sharding import PartitionSpec as P
 
 PATCH_X = 8
@@ -109,21 +111,210 @@
     return jnp.broadcast_to(within[:, None, None], (row_total,) + tuple(plane_shape))
 
 
-def contract_last(left, right):
+MESH = pl.DeviceIdType.MESH
+LANES = 128
+
+
+def dot_last(left, right):
     return lax.dot_general(
         left, right, (((1,), (1,)), ((), ())), preferred_element_type=jnp.float32
     )
 
 
-def contract_first(left, right):
-    return lax.dot_general(
-        left, right, (((0,), (0,)), ((), ())), preferred_element_type=jnp.float32
-    )
+def ring_place(dev, size):
+    odd = dev % 2
+    return (1 - odd) * (dev // 2) + odd * (size - 1 - dev // 2)
+
+
+def ring_dev(place, size):
+    back = place // (size // 2)
+    return (1 - back) * (2 * place) + back * (2 * (size - 1 - place) + 1)
+
+
+def scatter_kernel(
+    size, scale, up_cut, embed_cut,
+    act_ref, normed_ref, embed_ref, patch_ref, up_out, embed_out,
+    own_up, own_em, pair_out_up, pair_out_em, pair_in_up, pair_in_em,
+    ring_out_up, ring_out_em, ring_in_up, ring_in_em,
+    pair_send, pair_recv, ring_send, ring_recv,
+):
+    dev = lax.axis_index("dev")
+    core = lax.axis_index("rve")
+    place = ring_place(dev, size)
+    right = ring_dev((place + 1) % size, size)
+    left = ring_dev((place + size - 1) % size, size)
+    barrier = pltpu.get_barrier_semaphore()
+    pl.semaphore_signal(barrier, inc=1, device_id={"dev": right}, device_id_type=MESH)
+    pl.semaphore_signal(barrier, inc=1, device_id={"dev": left}, device_id_type=MESH)
+    pl.semaphore_signal(barrier, inc=1, device_id={"rve": 1 - core}, device_id_type=MESH)
+    pl.semaphore_wait(barrier, 3)
+    sides = (
+        (slice(0, up_cut), slice(0, embed_cut)),
+        (slice(up_cut, None), slice(embed_cut, None)),
+    )
+
+    def pair_copies(step):
+        return [
+            pltpu.make_async_remote_copy(
+                src_ref=source.at[step], dst_ref=target.at[step],
+                send_sem=pair_send.at[kind, step], recv_sem=pair_recv.at[kind, step],
+                device_id={"rve": 1 - core}, device_id_type=MESH,
+            )
+            for kind, (source, target) in enumerate(
+                ((pair_out_up, pair_in_up), (pair_out_em, pair_in_em))
+            )
+        ]
+
+    def ring_copies(step):
+        copies = []
+        for side, neighbour in enumerate((right, left)):
+            for kind, (source, target) in enumerate(
+                ((ring_out_up, ring_in_up), (ring_out_em, ring_in_em))
+            ):
+                cut = sides[side][kind]
+                copies.append(
+                    pltpu.make_async_remote_copy(
+                        src_ref=source.at[step, :, cut], dst_ref=target.at[step, :, cut],
+                        send_sem=ring_send.at[2 * side + kind, step],
+                        recv_sem=ring_recv.at[2 * side + kind, step],
+                        device_id={"dev": neighbour}, device_id_type=MESH,
+                    )
+                )
+        return copies
+
+    def compute(step):
+        blocks = ((place + 2 * size - 1 - step) % size, (place + 1 + step) % size)
+        for other in (True, False):
+            for side in range(2):
+                up_cols, em_cols = sides[side]
+                block = ring_dev(blocks[side], size) * 2 + ((1 - core) if other else core)
+                up = dot_last(act_ref[block], normed_ref[up_cols])
+                em = dot_last(embed_ref[block], patch_ref[em_cols])
+                if other:
+                    pair_out_up[step, :, up_cols] = up.astype(jnp.bfloat16)
+                    pair_out_em[step, :, em_cols] = em.astype(jnp.bfloat16)
+                else:
+                    own_up[step % 2, :, up_cols] = up
+                    own_em[step % 2, :, em_cols] = em
+            if other:
+                for copy in pair_copies(step):
+                    copy.start()
+
+    def finish(step, first, last):
+        for copy in pair_copies(step):
+            copy.wait_recv()
+        up = own_up[step % 2] + pair_in_up[step].astype(jnp.float32)
+        em = own_em[step % 2] + pair_in_em[step].astype(jnp.float32)
+        if not first:
+            for copy in ring_copies(step - 1):
+                copy.wait_recv()
+            up = up + ring_in_up[step - 1].astype(jnp.float32)
+            em = em + ring_in_em[step - 1].astype(jnp.float32)
+        if last:
+            up_out[...] = up * scale
+            embed_out[...] = em * scale
+        else:
+            ring_out_up[step] = up.astype(jnp.bfloat16)
+            ring_out_em[step] = em.astype(jnp.bfloat16)
+            for copy in ring_copies(step):
+                copy.start()
+
+    compute(0)
+    compute(1)
+    finish(0, True, False)
+
+    def body(step, carry):
+        compute(step + 1)
+        finish(step, False, False)
+        return carry
+
+    lax.fori_loop(1, size - 1, body, 0)
+    finish(size - 1, False, True)
+
+    def drain(step, carry):
+        for copy in pair_copies(step):
+            copy.wait_send()
+        return carry
+
+    def drain_ring(step, carry):
+        for copy in ring_copies(step):
+            copy.wait_send()
+        return carry
+
+    lax.fori_loop(0, size, drain, 0)
+    lax.fori_loop(0, size - 1, drain_ring, 0)
+
+
+def scatter_grads(act, normed, embed, patches, scale, size):
+    up_rows, em_rows = act.shape[1], embed.shape[1]
+    width, features = normed.shape[0], patches.shape[0]
+    up_cut = (width // LANES + 1) // 2 * LANES
+    embed_cut = features // LANES // 3 * LANES
+    wide = jnp.bfloat16
+    return pl.pallas_call(
+        partial(scatter_kernel, size, scale, up_cut, embed_cut),
+        out_shape=(
+            jax.ShapeDtypeStruct((up_rows, width), jnp.float32),
+            jax.ShapeDtypeStruct((em_rows, features), jnp.float32),
+        ),
+        in_specs=[pl.BlockSpec(memory_space=pltpu.VMEM)] * 4,
+        out_specs=(pl.BlockSpec(memory_space=pltpu.VMEM),) * 2,
+        scratch_shapes=[
+            pltpu.VMEM((2, up_rows, width), jnp.float32),
+            pltpu.VMEM((2, em_rows, features), jnp.float32),
+            *[
+                pltpu.VMEM(shape, wide)
+                for _ in range(4)
+                for shape in ((size, up_rows, width), (size, em_rows, features))
+            ],
+            pltpu.SemaphoreType.DMA((2, size)),
+            pltpu.SemaphoreType.DMA((2, size)),
+            pltpu.SemaphoreType.DMA((4, size)),
+            pltpu.SemaphoreType.DMA((4, size)),
+        ],
+        compiler_params=pltpu.CompilerParams(
+            collective_id=0, has_side_effects=True, vmem_limit_bytes=58 * 1024 * 1024
+        ),
+        cost_estimate=pl.CostEstimate(
+            flops=4 * size * patches.shape[1] * (up_rows * width + em_rows * features),
+            bytes_accessed=20_000_000,
+            transcendentals=0,
+        ),
+    )(act, normed, embed, patches)
 
 
 def gelu_grad(pre_act, cotangent):
     _, pullback = jax.vjp(partial(jax.nn.gelu, approximate=True), pre_act)
     return pullback(cotangent.astype(jnp.float32))[0].astype(jnp.bfloat16)
+
+
+def learner(patches, embed_all, up_all, cotangent, dev_count, rve_count):
+    tokens = patches.shape[1]
+    shards = dev_count * rve_count
+    grad_scale = 1.0 / math.sqrt(tokens * shards)
+    embedded = jnp.dot(embed_all, patches, preferred_element_type=jnp.float32).astype(jnp.bfloat16)
+    embed_wide = embedded.astype(jnp.float32)
+    inverse_rms = lax.rsqrt(jnp.mean(embed_wide * embed_wide, axis=0, keepdims=True) + epsilon)
+    normed_wide = embed_wide * inverse_rms
+    normed = normed_wide.astype(jnp.bfloat16)
+    pre_act = jnp.dot(up_all, normed, preferred_element_type=jnp.float32)
+    act_grad = gelu_grad(pre_act, cotangent)
+    normed_grad = lax.dot_general(
+        up_all, act_grad, (((0,), (0,)), ((), ())), preferred_element_type=jnp.float32
+    )
+    embed_in_grad = (
+        inverse_rms
+        * (normed_grad - normed_wide * jnp.mean(normed_grad * normed_wide, axis=0, keepdims=True))
+    ).astype(jnp.bfloat16)
+    grad_up, grad_embed = scatter_grads(
+        act_grad.reshape(shards, -1, tokens),
+        normed,
+        embed_in_grad.reshape(shards, -1, tokens),
+        patches,
+        grad_scale,
+        dev_count,
+    )
+    return (grad_embed, grad_up)
 
 
 def local(phase, load_case, moduli, loading_table, w_embed, w_up, cotangent):
@@ -157,38 +348,14 @@
         3, grid_x // PATCH_X, PATCH_X, band_rows // PATCH_Y, PATCH_Y, nz_cells // PATCH_Z, PATCH_Z
     )
     patches = cells.transpose(3, 1, 5, 0, 2, 4, 6).reshape(-1, 3 * PATCH_X * PATCH_Y * PATCH_Z)
-    token_count = patches.shape[0]
-    grad_scale = 1.0 / math.sqrt(token_count * dev_count * rve_count)
-    embedded = contract_last(
-        patches, lax.all_gather(w_embed, ("dev", "rve"), axis=0, tiled=True)
-    ).astype(jnp.bfloat16)
-    embed_wide = embedded.astype(jnp.float32)
-    inverse_rms = lax.rsqrt(jnp.mean(embed_wide * embed_wide, axis=-1, keepdims=True) + epsilon)
-    normed_wide = embed_wide * inverse_rms
-    normed = normed_wide.astype(jnp.bfloat16)
-    up_all = lax.all_gather(w_up, ("dev", "rve"), axis=0, tiled=True)
-    pre_act = contract_last(normed, up_all)
-    act_grad = gelu_grad(pre_act, cotangent)
-    columns = act_grad
-    grad_up = (
-        lax.psum_scatter(
-            contract_first(columns, normed), ("dev", "rve"), scatter_dimension=0, tiled=True
-        )
-        * grad_scale
-    )
-    normed_grad = jnp.dot(act_grad, up_all, preferred_element_type=jnp.float32)
-    embed_in_grad = (
-        inverse_rms
-        * (normed_grad - normed_wide * jnp.mean(normed_grad * normed_wide, axis=-1, keepdims=True))
-    ).astype(jnp.bfloat16)
-    columns = embed_in_grad
-    grad_embed = (
-        lax.psum_scatter(
-            contract_first(columns, patches), ("dev", "rve"), scatter_dimension=0, tiled=True
-        )
-        * grad_scale
-    )
-    return (displace[None], grad_embed, grad_up)
+    return (displace[None],) + learner(
+        patches.T,
+        lax.all_gather(w_embed, ("dev", "rve"), axis=0, tiled=True),
+        lax.all_gather(w_up, ("dev", "rve"), axis=0, tiled=True),
+        cotangent.T,
+        dev_count,
+        rve_count,
+    )
 
 
 def solution(mesh):

time: 486 us -> 308 us (0.63)
  waiting for transfers between devices: 268 us -> 57.8 us
  Pallas kernels: 0 us -> 70 us
  blocking collectives: 42.6 us -> 0 us
  local copies, waits for them, and re-layouts: 64.5 us -> 73.5 us
  matrix products: 35.4 us -> 26.9 us
  starting transfers between devices: 6.98 us -> 13 us
    reduce_scatter x2 -> x0, waiting for transfers between devices: 245 us -> none  [the longest x1 185 us: local(): lax.psum_scatter(contract_first(columns, normed), ('dev', 'rve'), scatter...]
    pallas_call x0 -> x1, Pallas kernels: none -> 70 us  [scatter_grads(): pl.pallas_call(partial(scatter_kernel, size, scale, up_cut, embed_cut), o...]
    all_to_all x1 -> x0, blocking collectives: 42.6 us -> none  [local(): lax.all_to_all(blocks, 'dev', split_axis=2, concat_axis=1, tiled=True)]
    all_to_all x0 -> x1, waiting for transfers between devices: none -> 35.4 us  [local(): lax.all_to_all(blocks, 'dev', split_axis=2, concat_axis=1, tiled=True)]
    ppermute x1, waiting for transfers between devices: 9.97 us -> 0.01 us  [with_halo(): after = lax.ppermute(initial, axis, down)]
    ppermute x1, waiting for transfers between devices: 11.4 us -> 21.1 us  [with_halo(): before = lax.ppermute(last, axis, up)]
    dot_general x5 -> x3, matrix products: 35.4 us -> 26.9 us  [the longest x1 14.8 us: learner(): pre_act = jnp.dot(up_all, normed, preferred_element_type=jnp.float32)]
    all_to_all x0 -> x1, starting transfers between devices: none -> 6.73 us  [local(): lax.all_to_all(blocks, 'dev', split_axis=2, concat_axis=1, tiled=True)]
  transfers between devices with their start and end apart: 6 -> 5, of which waited for: 4 -> 2; matrix products, arithmetic and copies ran while one was open for 26% -> 38% of each run, Pallas kernels for 0% -> 0%
where the time goes in v1:
time: 308 us; the launch traced here: 306 us
  local copies, waits for them, and re-layouts  73.5 us (24%)
  Pallas kernels  70 us (23%)
  waiting for transfers between devices  57.8 us (19%)
  other arithmetic  49.9 us (16%)
  matrix products  26.9 us (9%)
  between operations  15 us (5%)
  starting transfers between devices  13 us (4%)
    pallas_call x1, Pallas kernels, scatter_grads(): pl.pallas_call(partial(scatter_kernel, size, scale, up_cut, embed_cut), o...  70 us
    all_to_all x1, waiting for transfers between devices, local(): lax.all_to_all(blocks, 'dev', split_axis=2, concat_axis=1, tiled=True)  35.4 us
    another operation x11, other arithmetic, jacobi_sweep(): return jnp.stack(results)  31 us
    transpose x1, local copies, waits for them, and re-layouts, local(): cells.transpose(3, 1, 5, 0, 2, 4, 6)  29.5 us
    reshape x1, local copies, waits for them, and re-layouts, local(): regrouped.reshape(3, grid_x // PATCH_X, PATCH_X, band_rows // PATCH_Y, PA...  21.6 us
    ppermute x1, waiting for transfers between devices, with_halo(): before = lax.ppermute(last, axis, up)  21.1 us
    dot_general x1, matrix products, learner(): pre_act = jnp.dot(up_all, normed, preferred_element_type=jnp.float32)  14.8 us
    another operation x4, other arithmetic, first_iterate(): jnp.stack([jnp.where(inside, forcing / diagonal, 0.0) for face_list, forc...  13.4 us
  transfers between devices with their start and end apart: 5, of which 2 were waited for; matrix products, arithmetic and copies ran while one was open for 38% of the time, Pallas kernels for 0%

profile of v1, /device:TPU:0, one launch (start us, length us, event | category | flops | bytes accessed | tf_op | source)
XLA Modules:
  0.0 306.0 jit_solution(8123096878746844078)
XLA Ops:
  11.0 4.9 %collective-permute-start = (f32[2,4,128,128]{3,2,1,0:T(8,128)S(1)}, f32[2,4,128,128]{3,2,1,0:T(8,128)S(1)}, u32[]{:S(2)}, u32[]{:S(2)}) collective-permute-start(f32[2,4,128,128]{3,2,1,0:T(8,128)S(1)} %get-tuple-element.35), channel_id=1, source_target_pairs={{0,2},{2,4},{4,6},{6,8},{8,10},{10,12},{12,14},{1,3},{3,5},{5,7},{... | collective-permute-start | bytes 1572872 | tf_op jit(solution)/shard_map/ppermute | solution.py:27
  18.7 21.1 %collective-permute-done = f32[2,4,128,128]{3,2,1,0:T(8,128)S(1)} collective-permute-done((f32[2,4,128,128]{3,2,1,0:T(8,128)S(1)}, f32[2,4,128,128]{3,2,1,0:T(8,128)S(1)}, u32[]{:S(2)}, u32[]{:S(2)}) %collective-permute-start) | collective-permute-done | bytes 524320 | tf_op jit(solution)/shard_map/ppermute | solution.py:27
  40.3 5.1 %select_bitcast_fusion.11 = (f32[1,16,128,128]{3,2,1,0:T(8,128)S(1)}, f32[16,128,128]{2,1,0:T(8,128)S(1)}, f32[16,128,128]{2,1,0:T(8,128)S(1)}, f32[16,128,128]{...) fusion(f32[]{:T(128)} %bitcast.10, f32[]{:T(128)} %bitcast.8, ...), kind=kLoop, calls=%fused_computation.273 | loop fusion | flops 13893632 | bytes 9699356 | tf_op jit(solution)/shard_map/stack | solution.py:83
  45.4 4.3 %select_bitcast_fusion.10 = (f32[1,16,128,128]{3,2,1,0:T(8,128)S(1)}, f32[16,128,128]{2,1,0:T(8,128)S(1)}, f32[16,128,128]{2,1,0:T(8,128)S(1)}, f32[16,128,128]{2,1,0:T(8,128)S(1)}, f32[16,128,128]{2,1,0:T(8,128)S(1)}) fusion(f32[16,128,128]{2,1,0:T(8,128)S(1)} %get-tuple-element.13, f32[16,128,128]{2,1,0:T(8,128)S(1)} %get-tuple-element.12, f32[]{:T(128)} %bitcast.14, ...), kind=kLoop, calls=%fused_computation.264 | loop fusion | flops 10747904 | bytes 9699356 | tf_op jit(solution)/shard_map/stack | solution.py:83
  49.7 3.5 %select_bitcast_fusion.9 = (f32[1,16,128,128]{3,2,1,0:T(8,128)S(1)}, f32[16,128,128]{2,1,0:T(8,128)S(1)}, f32[16,128,128]{2,1,0:T(8,128)S(1)}) fusion(f32[16,128,128]{2,1,0:T(8,128)S(1)} %get-tuple-element.15, f32[16,128,128]{2,1,0:T(8,128)S(1)} %get-tuple-element.14, f32[16,128,128]{2,1,0:T(8,128)S(1)} %get-tuple-element.20, ...), kind=kLoop, calls=%fused_computation.255 | loop fusion | flops 7340032 | bytes 8650780 | tf_op jit(solution)/shard_map/stack | solution.py:83
  54.1 3.3 %select_bitcast_fusion.8 = f32[1,16,128,128]{3,2,1,0:T(8,128)S(1)} fusion(f32[16,128,128]{2,1,0:T(8,128)S(1)} %get-tuple-element.12, f32[16,128,128]{2,1,0:T(8,128)S(1)} %get-tuple-element.13, f32[16,128,128]{2,1,0:T(8,128)S(1)} %get-tuple-element.14, f32[16,128,128]{2,1,0:T(8,128)S(1)} %get-tuple-element.15, f32[16,128,128]{2,1,0:T(8,128)S(1)} %get-tuple-element.11, ...), kind=kLoop, calls=%fused_computation.254 | loop fusion | flops 7077888 | bytes 10616860 | tf_op jit(solution)/shard_map/stack | solution.py:105
  57.4 3.3 %select_bitcast_fusion.7 = f32[1,16,128,128]{3,2,1,0:T(8,128)S(1)} fusion(f32[16,128,128]{2,1,0:T(8,128)S(1)} %get-tuple-element.12, f32[18,128,128]{2,1,0:T(8,128)S(1)} %get-tuple-element.31, f32[16,128,128]{2,1,0:T(8,128)S(1)} %get-tuple-element.13, f32[16,128,128]{2,1,0:T(8,128)S(1)} %get-tuple-element.17, f32[16,128,128]{2,1,0:T(8,128)S(1)} %get-tuple-element.18, ...), kind=kLoop, calls=%fused_computation.253 | loop fusion | flops 7077888 | bytes 10616860 | tf_op jit(solution)/shard_map/stack | solution.py:105
  60.7 3.5 %select_bitcast_fusion.6 = f32[1,16,128,128]{3,2,1,0:T(8,128)S(1)} fusion(f32[16,128,128]{2,1,0:T(8,128)S(1)} %get-tuple-element.23, f32[18,128,128]{2,1,0:T(8,128)S(1)} %get-tuple-element.32, f32[16,128,128]{2,1,0:T(8,128)S(1)} %get-tuple-element.22, f32[16,128,128]{2,1,0:T(8,128)S(1)} %get-tuple-element.14, f32[16,128,128]{2,1,0:T(8,128)S(1)} %get-tuple-element.15, ...), kind=kLoop, calls=%fused_computation.252 | loop fusion | flops 7077888 | bytes 10616860 | tf_op jit(solution)/shard_map/stack | solution.py:105
  65.1 3.3 %select_bitcast_fusion.5 = f32[1,16,128,128]{3,2,1,0:T(8,128)S(1)} fusion(f32[16,128,128]{2,1,0:T(8,128)S(1)} %get-tuple-element.12, f32[16,128,128]{2,1,0:T(8,128)S(1)} %get-tuple-element.13, f32[16,128,128]{2,1,0:T(8,128)S(1)} %get-tuple-element.14, f32[16,128,128]{2,1,0:T(8,128)S(1)} %get-tuple-element.15, f32[16,128,128]{2,1,0:T(8,128)S(1)} %get-tuple-element.11, ...), kind=kLoop, calls=%fused_computation.251 | loop fusion | flops 7077888 | bytes 10616860 | tf_op jit(solution)/shard_map/stack | solution.py:105
  68.3 3.3 %select_bitcast_fusion.4 = f32[1,16,128,128]{3,2,1,0:T(8,128)S(1)} fusion(f32[16,128,128]{2,1,0:T(8,128)S(1)} %get-tuple-element.12, f32[18,128,128]{2,1,0:T(8,128)S(1)} %get-tuple-element.28, f32[16,128,128]{2,1,0:T(8,128)S(1)} %get-tuple-element.13, f32[16,128,128]{2,1,0:T(8,128)S(1)} %get-tuple-element.17, f32[16,128,128]{2,1,0:T(8,128)S(1)} %get-tuple-element.18, ...), kind=kLoop, calls=%fused_computation.250 | loop fusion | flops 7077888 | bytes 10616860 | tf_op jit(solution)/shard_map/stack | solution.py:105
  71.6 3.5 %select_bitcast_fusion.3 = f32[1,16,128,128]{3,2,1,0:T(8,128)S(1)} fusion(f32[16,128,128]{2,1,0:T(8,128)S(1)} %get-tuple-element.23, f32[18,128,128]{2,1,0:T(8,128)S(1)} %get-tuple-element.29, f32[16,128,128]{2,1,0:T(8,128)S(1)} %get-tuple-element.22, f32[16,128,128]{2,1,0:T(8,128)S(1)} %get-tuple-element.14, f32[16,128,128]{2,1,0:T(8,128)S(1)} %get-tuple-element.15, ...), kind=kLoop, calls=%fused_computation.249 | loop fusion | flops 7077888 | bytes 10616860 | tf_op jit(solution)/shard_map/stack | solution.py:105
  76.0 3.3 %select_bitcast_fusion.2 = f32[1,16,128,128]{3,2,1,0:T(8,128)S(1)} fusion(f32[16,128,128]{2,1,0:T(8,128)S(1)} %get-tuple-element.12, f32[16,128,128]{2,1,0:T(8,128)S(1)} %get-tuple-element.13, f32[16,128,128]{2,1,0:T(8,128)S(1)} %get-tuple-element.14, f32[16,128,128]{2,1,0:T(8,128)S(1)} %get-tuple-element.15, f32[16,128,128]{2,1,0:T(8,128)S(1)} %get-tuple-element.11, ...), kind=kLoop, calls=%fused_computation.248 | loop fusion | flops 7077888 | bytes 10616860 | tf_op jit(solution)/shard_map/stack | solution.py:105
  79.3 3.3 %select_bitcast_fusion.1 = f32[1,16,128,128]{3,2,1,0:T(8,128)S(1)} fusion(f32[16,128,128]{2,1,0:T(8,128)S(1)} %get-tuple-element.12, f32[18,128,128]{2,1,0:T(8,128)S(1)} %get-tuple-element.25, f32[16,128,128]{2,1,0:T(8,128)S(1)} %get-tuple-element.13, f32[16,128,128]{2,1,0:T(8,128)S(1)} %get-tuple-element.17, f32[16,128,128]{2,1,0:T(8,128)S(1)} %get-tuple-element.18, ...), kind=kLoop, calls=%fused_computation.247 | loop fusion | flops 7077888 | bytes 10616860 | tf_op jit(solution)/shard_map/stack | solution.py:105
  82.6 3.5 %select_bitcast_fusion = f32[1,16,128,128]{3,2,1,0:T(8,128)S(1)} fusion(f32[16,128,128]{2,1,0:T(8,128)S(1)} %get-tuple-element.23, f32[18,128,128]{2,1,0:T(8,128)S(1)} %get-tuple-element.26, f32[16,128,128]{2,1,0:T(8,128)S(1)} %get-tuple-element.22, f32[16,128,128]{2,1,0:T(8,128)S(1)} %get-tuple-element.14, f32[16,128,128]{2,1,0:T(8,128)S(1)} %get-tuple-element.15, ...), kind=kLoop, calls=%fused_computation.246 | loop fusion | flops 7077888 | bytes 10616860 | tf_op jit(solution)/shard_map/stack | solution.py:105
  87.3 6.7 %all-to-all-start = ((bf16[3,8,8,16,128]{4,3,1,0,2:T(8,128)(2,1)}), bf16[3,8,8,16,128]{4,3,1,0,2:T(8,128)(2,1)}, u32[]{:S(2)}, u32[]{:S(2)}) async-start(bf16[3,8,8,16,128]{4,3,1,0,2:T(8,128)(2,1)} %copy.29), calls=%async_computation | async-start | bytes 1572864 | tf_op jit(solution)/shard_map/all_to_all | solution.py:345
  95.3 35.4 %all-to-all-done = bf16[3,8,8,16,128]{4,3,1,0,2:T(8,128)(2,1)} async-done(((bf16[3,8,8,16,128]{4,3,1,0,2:T(8,128)(2,1)}), bf16[3,8,8,16,128]{4,3,1,0,2:T(8,128)(2,1)}, u32[]{:S(2)}, u32[]{:S(2)}) %all-to-all-start) | async-done | bytes 786464 | tf_op jit(solution)/shard_map/all_to_all | solution.py:345
  130.7 6.1 %copy.30 = bf16[3,8,8,1,16,128]{4,5,2,1,0,3:T(8,128)(2,1)} copy(bf16[3,8,8,1,16,128]{5,4,2,0,1,3:T(8,128)(2,1)} %bitcast.60) | data formatting | bytes 1572864 | tf_op jit(solution)/shard_map/all_to_all | solution.py:345
  136.7 21.6 %reshape.67 = bf16[3,8,8,2,8,32,4]{4,3,6,5,2,1,0:T(2,128)(2,1)} reshape(bf16[3,8,8,1,16,128]{4,5,2,1,0,3:T(8,128)(2,1)} %copy.30) | data formatting | bytes 1572864 | tf_op jit(solution)/shard_map/reshape | solution.py:347
  158.3 29.5 %copy.31 = bf16[2,8,32,3,8,8,4]{2,1,0,6,5,4,3:T(8,128)(2,1)S(1)} copy(bf16[2,8,32,3,8,8,4]{5,0,6,2,4,1,3:T(2,128)(2,1)} %bitcast.311) | data formatting | bytes 1572864 | tf_op jit(solution)/shard_map/transpose | solution.py:350
  187.9 3.8 %reshape.68 = bf16[512,768]{0,1:T(8,128)(2,1)} reshape(bf16[2,8,32,3,8,8,4]{2,1,0,6,5,4,3:T(8,128)(2,1)S(1)} %copy.31) | data formatting | bytes 1572864 | tf_op jit(solution)/shard_map/reshape | solution.py:350
  195.0 14.8 %fusion.6 = bf16[3072,512]{0,1:T(8,128)(2,1)} fusion(bf16[512,3072]{1,0:T(8,128)(2,1)} %param.13, bf16[1408,512]{1,0:T(8,128)(2,1)S(1)} %fusion.15.normed_ref, bf16[3072,1408]{1,0:T(8,128)(2,1)} %all-gather.5.cloned.1.call-done), kind=kOutput, calls=%fused_computation.8 | convolution fusion | flops 4462215168 | bytes 16384000 | tf_op jit(solution)/shard_map/dot_general | solution.py:300
  209.8 4.7 %copy.33 = bf16[3072,512]{1,0:T(8,128)(2,1)} copy(bf16[3072,512]{0,1:T(8,128)(2,1)} %fusion.6) | data formatting | bytes 6291456 | tf_op jit(solution)/shard_map/convert_element_type | solution.py:288
  214.5 9.0 %fusion.16 = (f32[512]{0:T(512)S(1)}, f32[1408,512]{1,0:T(8,128)S(1)}) fusion(bf16[512,1408]{0,1:T(8,128)(2,1)S(1)} %get-tuple-element.49, f32[512]{0:T(512)S(1)} %add_rsqrt_fusion, bf16[3072,512]{0,1:T(8,128)(2,1)} %fusion.6, bf16[3072,1408]{1,0:T(8,128)(2,1)} %all-gather.5.cloned.1.call-done), kind=kOutput, calls=%fused_computation.86 | convolution fusion | flops 4432068096 | bytes 16125952 | tf_op jit(solution)/shard_map/dot_general | solution.py:302
  225.2 70.0 %shard_map.94 = (f32[192,1408]{1,0:T(8,128)}, f32[88,768]{1,0:T(8,128)}) custom-call(bf16[16,192,512]{2,1,0:T(8,128)(2,1)} %bitcast.316, bf16[1408,512]{1,0:T(8,128)(2,1)} %copy-done, bf16[16,88,512]{2,1,0:T(8,128)(2,1)} %bitcast.318, bf16[768,512]{1,0:T(8,128)(2,1)} %bitcast.319), custom_call_target="tpu_custom_call" | custom-call | flops 5536481280 | bytes 20000000 | tf_op jit(solution)/shard_map/pallas_call | solution.py:254
  (38 shorter events, 20.6 us)
Async XLA Ops:
  7.2 10.7 %copy-start.1 = (f32[6,3,3]{0,2,1:T(4,128)S(1)}, f32[6,3,3]{0,2,1:T(4,128)}, u32[]{:S(2)}) copy-start(f32[6,3,3]{0,2,1:T(4,128)} %param.10) | copy-start | bytes 652
  7.2 184.5 %all-gather.3.cloned.1.call-start = ((), (), s32[]{:S(2)}) async-start(), calls=%async_computation.1 | async-start | bytes 2297856 | tf_op jit(solution)/shard_map/all_gather | solution.py:353
  7.9 187.1 %all-gather.5.cloned.1.call-start = ((), (), s32[]{:S(2)}) async-start(), calls=%async_computation.2 | async-start | bytes 9191424 | tf_op jit(solution)/shard_map/all_gather | solution.py:354
  11.0 28.7 %collective-permute-start = (f32[2,4,128,128]{3,2,1,0:T(8,128)S(1)}, f32[2,4,128,128]{3,2,1,0:T(8,128)S(1)}, u32[]{:S(2)}, u32[]{:S(2)}) collective-permute-start(f32[2,4,128,128]{3,2,1,0:T(8,128)S(1)} %get-tuple-element.35), channel_id=1, source_target_pairs={{0,2},{2,4},{4,6},{6,8},{8,10},{10,12},{12,14},{1,3},{3,5},{5,7},{... | collective-permute-start | bytes 1572872 | tf_op jit(solution)/shard_map/ppermute | solution.py:27
  15.9 23.8 %collective-permute-start.1 = (f32[2,4,128,128]{3,2,1,0:T(8,128)S(1)}, f32[2,4,128,128]{3,2,1,0:T(8,128)S(1)}, u32[]{:S(2)}, u32[]{:S(2)}) collective-permute-start(f32[2,4,128,128]{3,2,1,0:T(8,128)S(1)} %get-tuple-element.36), channel_id=1, source_target_pairs={{2,0},{4,2},{6,4},{8,6},{10,8},{12,10},{14,12},{3,1},{5,3},{7,5},{... | collective-permute-start | bytes 1572872 | tf_op jit(solution)/shard_map/ppermute | solution.py:28
  87.3 43.4 %all-to-all-start = ((bf16[3,8,8,16,128]{4,3,1,0,2:T(8,128)(2,1)}), bf16[3,8,8,16,128]{4,3,1,0,2:T(8,128)(2,1)}, u32[]{:S(2)}, u32[]{:S(2)}) async-start(bf16[3,8,8,16,128]{4,3,1,0,2:T(8,128)(2,1)} %copy.29), calls=%async_computation | async-start | bytes 1572864 | tf_op jit(solution)/shard_map/all_to_all | solution.py:345
  195.0 14.8 %copy-start = (bf16[1408,512]{1,0:T(8,128)(2,1)}, bf16[1408,512]{1,0:T(8,128)(2,1)S(1)}, u32[]{:S(2)}) copy-start(bf16[1408,512]{1,0:T(8,128)(2,1)S(1)} %fusion.15.normed_ref) | copy-start | bytes 4325380
Sparse Core Ops, SparseCore 0:
  10.3 53.6 all-gather.2
  66.3 84.8 all-gather.4

commit v2 on v1

--- a/solution.py
+++ b/solution.py
@@ -15,100 +15,6 @@
 
 
 epsilon = 1e-06
-
-
-def with_halo(value, sides, width):
-    for axis, dim in sides:
-        size, length = (lax.axis_size(axis), value.shape[dim])
-        up = [(i, (i + 1) % size) for i in range(size - 1)]
-        down = [(j, i) for i, j in up]
-        last = lax.slice_in_dim(value, length - width, length, axis=dim)
-        initial = lax.slice_in_dim(value, 0, width, axis=dim)
-        before = lax.ppermute(last, axis, up)
-        after = lax.ppermute(initial, axis, down)
-        value = jnp.concatenate([before, value, after], axis=dim)
-    return value
-
-
-def stiffness(phase, moduli):
-    labels = jnp.arange(moduli.shape[1], dtype=jnp.int32)
-    member = (labels[:, None, None, None] == phase[None]).astype(jnp.float32)
-    shear_stiff = jnp.sum(member * moduli[0][:, None, None, None], axis=0)
-    axial_stiff = jnp.sum(member * moduli[1][:, None, None, None], axis=0)
-    return (shear_stiff, axial_stiff)
-
-
-def harmonic(here, there, in_here, in_there):
-    blended = 2.0 * here * there / (here + there)
-    return jnp.where(in_here & in_there, blended, jnp.where(in_here, here, there))
-
-
-def face_pairs(stiff, inside):
-    stiff = jnp.where(inside, stiff, 1.0)
-    padded = jnp.pad(stiff, 1, constant_values=1.0)
-    in_pad = jnp.pad(inside, 1)
-    face_list = []
-    for direction in range(3):
-        upper_cut = [slice(1, -1)] * 3
-        lower_cut = [slice(1, -1)] * 3
-        upper_cut[direction] = slice(2, None)
-        lower_cut[direction] = slice(0, -2)
-        upper_face = harmonic(stiff, padded[tuple(upper_cut)], inside, in_pad[tuple(upper_cut)])
-        lower_face = harmonic(stiff, padded[tuple(lower_cut)], inside, in_pad[tuple(lower_cut)])
-        face_list.append((upper_face, lower_face))
-    return face_list
-
-
-def operator_terms(shear_stiff, axial_stiff, inside, strain):
-    shear_faces = face_pairs(shear_stiff, inside)
-    axial_faces = face_pairs(axial_stiff, inside)
-    terms = []
-    for component in range(3):
-        face_list = [
-            axial_faces[direction] if direction == component else shear_faces[direction]
-            for direction in range(3)
-        ]
-        forcing = strain[component, 0] * (face_list[0][0] - face_list[0][1])
-        diagonal = face_list[0][0] + face_list[0][1]
-        for direction in (1, 2):
-            forcing = forcing + strain[component, direction] * (
-                face_list[direction][0] - face_list[direction][1]
-            )
-            diagonal = diagonal + face_list[direction][0] + face_list[direction][1]
-        terms.append((face_list, forcing, diagonal))
-    return terms
-
-
-def first_iterate(terms, inside):
-    return jnp.stack(
-        [jnp.where(inside, forcing / diagonal, 0.0) for face_list, forcing, diagonal in terms]
-    )
-
-
-def jacobi_sweep(ghosted, terms, inside):
-    results = []
-    for component in range(3):
-        face_list, forcing, diagonal = terms[component]
-        padded = jnp.pad(ghosted[component], ((0, 0), (1, 1), (1, 1)))
-        summed = forcing
-        for direction in range(3):
-            upper_cut = [slice(1, -1)] * 3
-            lower_cut = [slice(1, -1)] * 3
-            upper_cut[direction] = slice(2, None)
-            lower_cut[direction] = slice(0, -2)
-            summed = (
-                summed
-                + face_list[direction][0] * padded[tuple(upper_cut)]
-                + face_list[direction][1] * padded[tuple(lower_cut)]
-            )
-        results.append(jnp.where(inside, summed / diagonal, 0.0))
-    return jnp.stack(results)
-
-
-def row_mask(first_global, row_total, grid_rows, plane_shape):
-    global_rows = first_global + jnp.arange(row_total, dtype=jnp.int32)
-    within = (global_rows >= 0) & (global_rows < grid_rows)
-    return jnp.broadcast_to(within[:, None, None], (row_total,) + tuple(plane_shape))
 
 
 MESH = pl.DeviceIdType.MESH
@@ -286,6 +192,355 @@
 def gelu_grad(pre_act, cotangent):
     _, pullback = jax.vjp(partial(jax.nn.gelu, approximate=True), pre_act)
     return pullback(cotangent.astype(jnp.float32))[0].astype(jnp.bfloat16)
+
+
+def field_kernel(
+    size, grid_rows, phase_ref, inverse_ref, strain_ref, up_ref, em_ref,
+    disp_ref, patch_ref, up_all, em_all,
+    labels, face_x, face_y, face_z, forcing, scale_back, field, outgo, income, sorted_rows,
+    halo_send, halo_recv, ring_send, ring_recv, pair_send, pair_recv, own_sem, swap_send, swap_recv,
+):
+    slab, ny, nz = phase_ref.shape
+    width = SWEEPS
+    phases = inverse_ref.shape[1]
+    dev = lax.axis_index("dev")
+    core = lax.axis_index("rve")
+    place = ring_place(dev, size)
+    right = ring_dev((place + 1) % size, size)
+    left = ring_dev((place + size - 1) % size, size)
+    half = size // 2
+    up_cut = (up_ref.shape[1] // LANES + 1) // 2 * LANES
+    em_cut = em_ref.shape[1] // LANES // 3 * LANES
+
+    barrier = pltpu.get_barrier_semaphore()
+    for offset in range(1, size):
+        pl.semaphore_signal(
+            barrier, inc=1, device_id={"dev": (dev + offset) % size}, device_id_type=MESH
+        )
+    pl.semaphore_signal(barrier, inc=1, device_id={"rve": 1 - core}, device_id_type=MESH)
+    pl.semaphore_wait(barrier, size)
+
+    def halo(up):
+        if up:
+            source, target = phase_ref.at[pl.ds(slab - width, width)], labels.at[pl.ds(0, width)]
+        else:
+            source, target = phase_ref.at[pl.ds(0, width)], labels.at[pl.ds(width + slab, width)]
+        way = 0 if up else 1
+        return pltpu.make_async_remote_copy(
+            src_ref=source, dst_ref=target, send_sem=halo_send.at[way], recv_sem=halo_recv.at[way],
+            device_id={"dev": (dev + 1) % size if up else (dev + size - 1) % size},
+            device_id_type=MESH,
+        )
+
+    @pl.when(dev < size - 1)
+    def _():
+        halo(True).start()
+
+    @pl.when(dev > 0)
+    def _():
+        halo(False).start()
+
+    def index_of(spot):
+        return ring_dev((spot + 2 * size) % size, size) * 2 + core
+
+    def ring_copies(step):
+        copies = []
+        for side, neighbour in enumerate((right, left)):
+            spot = place - step if side == 0 else place + step
+            block = index_of(spot)
+            for kind, (mine, every, cut) in enumerate(
+                ((up_ref, up_all, up_cut), (em_ref, em_all, em_cut))
+            ):
+                source, target = mine if step == 0 else every.at[block], every.at[block]
+                if step == half - 1:
+                    cols = pl.ds(0, cut) if side == 0 else pl.ds(cut, mine.shape[1] - cut)
+                    source, target = source.at[:, cols], target.at[:, cols]
+                copies.append(
+                    pltpu.make_async_remote_copy(
+                        src_ref=source, dst_ref=target,
+                        send_sem=ring_send.at[2 * side + kind, step],
+                        recv_sem=ring_recv.at[2 * side + kind, step],
+                        device_id={"dev": neighbour}, device_id_type=MESH,
+                    )
+                )
+        return copies
+
+    def pair_copies(spot, slot):
+        block = index_of(spot)
+        return [
+            pltpu.make_async_remote_copy(
+                src_ref=mine if slot == 0 else every.at[block], dst_ref=every.at[block],
+                send_sem=pair_send.at[kind, slot], recv_sem=pair_recv.at[kind, slot],
+                device_id={"rve": 1 - core}, device_id_type=MESH,
+            )
+            for kind, (mine, every) in enumerate(((up_ref, up_all), (em_ref, em_all)))
+        ]
+
+    def own_copies():
+        block = index_of(place)
+        return [
+            pltpu.make_async_copy(mine, every.at[block], own_sem.at[kind])
+            for kind, (mine, every) in enumerate(((up_ref, up_all), (em_ref, em_all)))
+        ]
+
+    pair_list = [(0, 0)]
+    for step in range(half - 1):
+        pair_list += [(-1 - step, 1 + 2 * step), (1 + step, 2 + 2 * step)]
+    pair_list.append((half, 2 * half - 1))
+
+    def gather_step(step):
+        if step > 0:
+            for copy in ring_copies(step - 1):
+                copy.wait_recv()
+        if step < half:
+            for copy in ring_copies(step):
+                copy.start()
+        if step == 0:
+            fresh = pair_list[:1]
+        elif step < half:
+            fresh = pair_list[2 * step - 1 : 2 * step + 1]
+        else:
+            fresh = pair_list[-1:]
+        for shift, slot in fresh:
+            for copy in pair_copies(place + shift, slot):
+                copy.start()
+
+    gather_step(0)
+    for copy in own_copies():
+        copy.start()
+
+    labels[pl.ds(width, slab)] = phase_ref[...]
+
+    @pl.when(dev == 0)
+    def _():
+        for row in range(width):
+            labels[row] = phase_ref[0]
+
+    @pl.when(dev == size - 1)
+    def _():
+        for row in range(width):
+            labels[width + slab + row] = phase_ref[slab - 1]
+
+    @pl.when(dev > 0)
+    def _():
+        halo(True).wait_recv()
+
+    @pl.when(dev < size - 1)
+    def _():
+        halo(False).wait_recv()
+
+    y_at = lax.broadcasted_iota(jnp.int32, (ny, nz), 0)
+    z_at = lax.broadcasted_iota(jnp.int32, (ny, nz), 1)
+
+    def inverse(row, kind):
+        label = labels[row]
+        value = jnp.full((ny, nz), inverse_ref[kind, phases - 1], jnp.float32)
+        for phase in range(phases - 1):
+            value = jnp.where(label == phase, inverse_ref[kind, phase], value)
+        return value
+
+    def within(row):
+        spot = dev * slab - width + row
+        at = jnp.full((ny, nz), spot, jnp.int32)
+        return (at >= 0) & (at < grid_rows)
+
+    def terms_row(row, carry):
+        faces = []
+        for kind in range(2):
+            here = inverse(row, kind)
+            upper_x = 2.0 / (here + inverse(row + 1, kind))
+            lower_x = 2.0 / (here + inverse(row - 1, kind))
+            upper_y = 2.0 / (here + jnp.where(y_at == ny - 1, here, pltpu.roll(here, ny - 1, 0)))
+            lower_y = 2.0 / (here + jnp.where(y_at == 0, here, pltpu.roll(here, 1, 0)))
+            upper_z = 2.0 / (here + jnp.where(z_at == nz - 1, here, pltpu.roll(here, nz - 1, 1)))
+            lower_z = 2.0 / (here + jnp.where(z_at == 0, here, pltpu.roll(here, 1, 1)))
+            face_x[2 * kind, row] = upper_x
+            face_x[2 * kind + 1, row] = lower_x
+            face_y[2 * kind, row] = jnp.where(y_at == ny - 1, 0.0, upper_y)
+            face_y[2 * kind + 1, row] = jnp.where(y_at == 0, 0.0, lower_y)
+            face_z[2 * kind, row] = jnp.where(z_at == nz - 1, 0.0, upper_z)
+            face_z[2 * kind + 1, row] = jnp.where(z_at == 0, 0.0, lower_z)
+            faces.append(
+                [
+                    (upper - lower, upper + lower)
+                    for upper, lower in (
+                        (upper_x, lower_x), (upper_y, lower_y), (upper_z, lower_z)
+                    )
+                ]
+            )
+        inside = within(row)
+        for component in range(3):
+            force = 0.0
+            total = 0.0
+            for direction in range(3):
+                difference, both = faces[1 if direction == component else 0][direction]
+                force = force + strain_ref[component, direction] * difference
+                total = total + both
+            back = jnp.where(inside, 1.0 / total, 0.0)
+            forcing[component, row] = force
+            scale_back[component, row] = back
+            field[0, component, row] = force * back
+        return carry
+
+    def sweep(repeat):
+        source, target = repeat % 2, (repeat + 1) % 2
+        last = repeat == SWEEPS - 2
+
+        def sweep_row(row, carry):
+            for component in range(3):
+                kinds = [2 if direction == component else 0 for direction in range(3)]
+                here = field[source, component, row]
+                total = forcing[component, row]
+                total = total + face_x[kinds[0], row] * field[source, component, row + 1]
+                total = total + face_x[kinds[0] + 1, row] * field[source, component, row - 1]
+                total = total + face_y[kinds[1], row] * pltpu.roll(here, ny - 1, 0)
+                total = total + face_y[kinds[1] + 1, row] * pltpu.roll(here, 1, 0)
+                total = total + face_z[kinds[2], row] * pltpu.roll(here, nz - 1, 1)
+                total = total + face_z[kinds[2] + 1, row] * pltpu.roll(here, 1, 1)
+                result = total * scale_back[component, row]
+                if last:
+                    disp_ref[component, row - width] = result
+                else:
+                    field[target, component, row] = result
+            return carry
+
+        lax.fori_loop(2 + repeat, slab + 2 * width - 2 - repeat, sweep_row, 0)
+
+    lax.fori_loop(1, slab + 2 * width - 1, terms_row, 0)
+    gather_step(1)
+    sweep(0)
+    sweep(1)
+    gather_step(2)
+    sweep(2)
+
+    bands = ny // PATCH_Y // size
+    piece = 3 * slab * PATCH_Y
+
+    for dest in range(size):
+        for band in range(bands):
+            first = (dest * bands + band) * PATCH_Y
+            rows = disp_ref[:, :, first : first + PATCH_Y, :].reshape(piece, nz)
+            outgo[dest, band * piece : (band + 1) * piece] = rows.astype(jnp.bfloat16)
+
+    def swap_copy(offset):
+        dest = (dev + offset) % size
+        return pltpu.make_async_remote_copy(
+            src_ref=outgo.at[dest], dst_ref=income.at[dev],
+            send_sem=swap_send.at[offset], recv_sem=swap_recv.at[offset],
+            device_id={"dev": dest}, device_id_type=MESH,
+        )
+
+    for offset in range(1, size):
+        swap_copy(offset).start()
+    income[dev] = outgo[dev]
+    for step in range(3, half):
+        gather_step(step)
+    for offset in range(1, size):
+        swap_copy(offset).wait_recv()
+
+    cells = nz // PATCH_Z
+    joined = LANES // cells
+    depth = joined * nz
+    from_row = lax.broadcasted_iota(jnp.int32, (depth, LANES), 0)
+    to_lane = lax.broadcasted_iota(jnp.int32, (depth, LANES), 1)
+    base = (to_lane // cells) * nz + (to_lane % cells) * PATCH_Z
+    for band in range(bands):
+        for group in range(size // joined):
+            rows = jnp.concatenate(
+                [
+                    income[group * joined + member, band * piece : (band + 1) * piece]
+                    for member in range(joined)
+                ],
+                axis=1,
+            )
+            lane = band * size * cells + group * LANES
+            for part in range(PATCH_Z):
+                pick = jnp.where(from_row == base + part, 1.0, 0.0).astype(jnp.bfloat16)
+                sorted_rows[part * piece : (part + 1) * piece, lane : lane + LANES] = jnp.dot(
+                    rows, pick, preferred_element_type=jnp.float32
+                ).astype(jnp.bfloat16)
+    features = PATCH_Z * piece
+    to_row = lax.broadcasted_iota(jnp.int32, (features, features), 0)
+    from_col = lax.broadcasted_iota(jnp.int32, (features, features), 1)
+    order = (to_row % PATCH_Z) * piece + to_row // PATCH_Z
+    move = jnp.where(from_col == order, 1.0, 0.0).astype(jnp.bfloat16)
+    patch_ref[...] = jnp.dot(
+        move, sorted_rows[...], preferred_element_type=jnp.float32
+    ).astype(jnp.bfloat16)
+
+    gather_step(half)
+
+    @pl.when(dev < size - 1)
+    def _():
+        halo(True).wait_send()
+
+    @pl.when(dev > 0)
+    def _():
+        halo(False).wait_send()
+
+    for copy in own_copies():
+        copy.wait()
+    for step in range(half):
+        for copy in ring_copies(step):
+            copy.wait_send()
+    for shift, slot in pair_list:
+        for copy in pair_copies(place + shift, slot):
+            copy.wait()
+    for offset in range(1, size):
+        swap_copy(offset).wait_send()
+
+
+def fields_and_gathers(phase, inverse, strain, w_embed, w_up, size):
+    slab, ny, nz = phase.shape
+    rows = slab + 2 * SWEEPS
+    bands = ny // PATCH_Y // size
+    piece = 3 * slab * PATCH_Y
+    features = PATCH_Z * piece
+    tokens = bands * size * (nz // PATCH_Z)
+    wide = jnp.float32
+    half = size // 2
+    plane = (rows, ny, nz)
+    vmem = pl.BlockSpec(memory_space=pltpu.VMEM)
+    smem = pl.BlockSpec(memory_space=pltpu.SMEM)
+    far = pl.BlockSpec(memory_space=pl.ANY)
+    return pl.pallas_call(
+        partial(field_kernel, size, slab * size),
+        out_shape=(
+            jax.ShapeDtypeStruct((3, slab, ny, nz), wide),
+            jax.ShapeDtypeStruct((features, tokens), jnp.bfloat16),
+            jax.ShapeDtypeStruct((2 * size,) + w_up.shape, w_up.dtype),
+            jax.ShapeDtypeStruct((2 * size,) + w_embed.shape, w_embed.dtype),
+        ),
+        in_specs=[vmem, smem, smem, far, far],
+        out_specs=(vmem, vmem, far, far),
+        scratch_shapes=[
+            pltpu.VMEM(plane, jnp.int32),
+            pltpu.VMEM((4,) + plane, wide),
+            pltpu.VMEM((4,) + plane, wide),
+            pltpu.VMEM((4,) + plane, wide),
+            pltpu.VMEM((3,) + plane, wide),
+            pltpu.VMEM((3,) + plane, wide),
+            pltpu.VMEM((2, 3) + plane, wide),
+            pltpu.VMEM((size, bands * piece, nz), jnp.bfloat16),
+            pltpu.VMEM((size, bands * piece, nz), jnp.bfloat16),
+            pltpu.VMEM((features, tokens), jnp.bfloat16),
+            pltpu.SemaphoreType.DMA((2,)),
+            pltpu.SemaphoreType.DMA((2,)),
+            pltpu.SemaphoreType.DMA((4, half)),
+            pltpu.SemaphoreType.DMA((4, half)),
+            pltpu.SemaphoreType.DMA((2, size)),
+            pltpu.SemaphoreType.DMA((2, size)),
+            pltpu.SemaphoreType.DMA((2,)),
+            pltpu.SemaphoreType.DMA((size,)),
+            pltpu.SemaphoreType.DMA((size,)),
+        ],
+        compiler_params=pltpu.CompilerParams(
+            collective_id=1, has_side_effects=True, vmem_limit_bytes=58 * 1024 * 1024
+        ),
+        cost_estimate=pl.CostEstimate(
+            flops=2_000_000_000, bytes_accessed=30_000_000, transcendentals=0
+        ),
+    )(phase, inverse, strain, w_up, w_embed)
 
 
 def learner(patches, embed_all, up_all, cotangent, dev_count, rve_count):
@@ -318,40 +573,18 @@
 
 
 def local(phase, load_case, moduli, loading_table, w_embed, w_up, cotangent):
-    local_phase = phase[0]
-    slab_rows = local_phase.shape[0]
-    plane_shape = local_phase.shape[1:]
     dev_count = lax.axis_size("dev")
     rve_count = lax.axis_size("rve")
-    first_row = lax.axis_index("dev") * slab_rows
-    grid_rows = slab_rows * dev_count
-    shear_stiff, axial_stiff = stiffness(local_phase, moduli)
     case_labels = jnp.arange(loading_table.shape[0], dtype=jnp.int32)
     case_pick = (case_labels == load_case[0]).astype(jnp.float32)
     strain = jnp.sum(case_pick[:, None, None] * loading_table, axis=0)
-    stacked = jnp.stack([shear_stiff, axial_stiff])
-    ghosted = with_halo(stacked, (("dev", 1),), SWEEPS)
-    inside = row_mask(first_row - SWEEPS, slab_rows + 2 * SWEEPS, grid_rows, plane_shape)
-    terms = operator_terms(ghosted[0], ghosted[1], inside, strain)
-    displace = first_iterate(terms, inside)
-    for repeat in range(SWEEPS - 1):
-        displace = jacobi_sweep(jnp.pad(displace, ((0, 0), (1, 1), (0, 0), (0, 0))), terms, inside)
-    displace = displace[:, SWEEPS : SWEEPS + slab_rows]
-    rounded = displace.astype(jnp.bfloat16)
-    ny_cells = rounded.shape[2]
-    nz_cells = rounded.shape[3]
-    band_rows = ny_cells // dev_count
-    blocks = rounded.reshape(3, slab_rows, dev_count, band_rows, nz_cells)
-    regrouped = lax.all_to_all(blocks, "dev", split_axis=2, concat_axis=1, tiled=True)
-    grid_x = regrouped.shape[1]
-    cells = regrouped.reshape(
-        3, grid_x // PATCH_X, PATCH_X, band_rows // PATCH_Y, PATCH_Y, nz_cells // PATCH_Z, PATCH_Z
+    displace, patches, up_all, embed_all = fields_and_gathers(
+        phase[0], 1.0 / moduli, strain, w_embed, w_up, dev_count
     )
-    patches = cells.transpose(3, 1, 5, 0, 2, 4, 6).reshape(-1, 3 * PATCH_X * PATCH_Y * PATCH_Z)
     return (displace[None],) + learner(
-        patches.T,
-        lax.all_gather(w_embed, ("dev", "rve"), axis=0, tiled=True),
-        lax.all_gather(w_up, ("dev", "rve"), axis=0, tiled=True),
+        patches,
+        embed_all.reshape(-1, w_embed.shape[1]),
+        up_all.reshape(-1, w_up.shape[1]),
         cotangent.T,
         dev_count,
         rve_count,

time: 308 us -> 192 us (0.62)
  Pallas kernels: 70 us -> 161 us
  local copies, waits for them, and re-layouts: 73.5 us -> 7.14 us
  waiting for transfers between devices: 57.8 us -> 0 us
  other arithmetic: 49.9 us -> 4.65 us
  between operations: 15 us -> 1.41 us
  starting transfers between devices: 13 us -> 0 us
  matrix products: 26.9 us -> 17.7 us
    pallas_call x0 -> x1, Pallas kernels: none -> 89.1 us  [fields_and_gathers(): pl.pallas_call(partial(field_kernel, size, slab * size), out_shape=(jax.S...]
    another operation x16 -> x0, other arithmetic: 44.5 us -> none  [the longest x11 31 us: jacobi_sweep(): return jnp.stack(results)]
    all_to_all x1 -> x0, waiting for transfers between devices: 35.4 us -> none  [local(): lax.all_to_all(blocks, 'dev', split_axis=2, concat_axis=1, tiled=True)]
    transpose x1 -> x0, local copies, waits for them, and re-layouts: 29.5 us -> none  [local(): cells.transpose(3, 1, 5, 0, 2, 4, 6)]
    reshape x3 -> x0, local copies, waits for them, and re-layouts: 26.5 us -> none  [the longest x1 21.6 us: local(): regrouped.reshape(3, grid_x // PATCH_X, PATCH_X, band_rows // PATCH_Y, PA...]
    ppermute x2 -> x0, waiting for transfers between devices: 21.1 us -> none  [the longest x1 21.1 us: with_halo(): before = lax.ppermute(last, axis, up)]
    all_to_all x1 -> x0, starting transfers between devices: 6.73 us -> none  [local(): lax.all_to_all(blocks, 'dev', split_axis=2, concat_axis=1, tiled=True)]
    ppermute x2 -> x0, starting transfers between devices: 6.2 us -> none  [the longest x1 4.9 us: with_halo(): before = lax.ppermute(last, axis, up)]
  transfers between devices with their start and end apart: 5 -> 0, of which waited for: 2 -> 0; matrix products, arithmetic and copies ran while one was open for 38% -> 0% of each run, Pallas kernels for 0% -> 0%
where the time goes in v2:
time: 192 us
  Pallas kernels  161 us (84%)
  matrix products  17.7 us (9%)
  local copies, waits for them, and re-layouts  7.14 us (4%)
  other arithmetic  4.65 us (2%)
    pallas_call x1, Pallas kernels, fields_and_gathers(): pl.pallas_call(partial(field_kernel, size, slab * size), out_shape=(jax.S...  89.1 us
    pallas_call x1, Pallas kernels, scatter_grads(): pl.pallas_call(partial(scatter_kernel, size, scale, up_cut, embed_cut), o...  72.1 us
    dot_general x1, matrix products, learner(): pre_act = jnp.dot(up_all, normed, preferred_element_type=jnp.float32)  9.48 us
    unnamed x16, local copies, waits for them, and re-layouts  7.14 us
    dot_general x1, matrix products, learner(): lax.dot_general(up_all, act_grad, (((0,), (0,)), ((), ())), preferred_ele...  4.95 us

profile of v2, /device:TPU:0, one launch (start us, length us, event | category | flops | bytes accessed | tf_op | source)
XLA Modules:
  0.0 192.0 jit_solution(5708351617632420361)
XLA Ops:
  1.3 1.2 broadcast_divide_fusion.inverse_ref
  2.5 1.4 multiply_reduce_fusion.strain_ref
  3.9 3.2 %copy.10 = bf16[512,3072]{0,1:T(8,128)(2,1)S(1)} copy(bf16[512,3072]{1,0:T(8,128)(2,1)} %param.13) | data formatting | bytes 6291456 | tf_op args[6]
  7.1 89.1 %shard_map.94 = (f32[3,8,128,128]{3,2,1,0:T(8,128)}, bf16[768,512]{1,0:T(8,128)(2,1)}, bf16[16,192,1408]{2,1,0:T(8,128)(2,1)}, bf16[16,88,768]{2,1,0:T(8,128)(2,1)}) custom-call(s32[8,128,128]{2,1,0:T(8,128)} %bitcast.29, f32[2,3]{1,0:T(2,128)} %broadcast_divide_fusion.inverse_ref, f32[3,3]{1,0:T(4,128)} %multiply_reduce_fusion.strain_ref, ...), custom_call_target="tpu_custom_call" | custom-call | flops 2000000000 | bytes 30000000 | tf_op jit(solution)/shard_map/pallas_call | solution.py:506
  96.2 0.0 copy-start.4
  96.2 3.2 %fusion.17 = (f32[512]{0:T(512)S(1)}, bf16[1408,512]{1,0:T(8,128)(2,1)S(1)}) fusion(bf16[1408,768]{1,0:T(8,128)(2,1)} %bitcast.33, bf16[768,512]{1,0:T(8,128)(2,1)} %get-tuple-element.12.patch_ref), kind=kOutput, calls=%fused_computation.24 | convolution fusion | flops 1110179328 | bytes 4392960 | tf_op jit(solution)/shard_map/dot_general | solution.py:550
  99.4 0.3 fusion.12.normed_ref
  99.8 0.0 copy-start.1
  99.8 1.1 copy-done.1
  100.9 0.0 copy-done.4
  100.9 9.5 %fusion.6 = bf16[3072,512]{1,0:T(8,128)(2,1)S(1)} fusion(bf16[512,3072]{0,1:T(8,128)(2,1)S(1)} %copy.10, bf16[3072,1408]{1,0:T(8,128)(2,1)S(1)} %bitcast.30, bf16[1408,512]{1,0:T(8,128)(2,1)S(1)} %fusion.12.normed_ref), kind=kOutput, calls=%fused_computation.8 | convolution fusion | flops 4462215168 | bytes 16384000 | tf_op jit(solution)/shard_map/dot_general | solution.py:555
  110.4 0.0 copy-start.5
  110.4 5.0 %fusion.13 = (f32[512]{0:T(512)S(1)}, f32[1408,512]{1,0:T(8,128)S(1)}) fusion(bf16[1408,512]{1,0:T(8,128)(2,1)S(1)} %get-tuple-element.16, f32[512]{0:T(512)S(1)} %add_rsqrt_fusion, bf16[3072,1408]{1,0:T(8,128)(2,1)S(1)} %bitcast.31, bf16[3072,512]{1,0:T(8,128)(2,1)S(1)} %fusion.6), kind=kOutput, calls=%fused_computation.20 | convolution fusion | flops 4432068096 | bytes 16125952 | tf_op jit(solution)/shard_map/dot_general | solution.py:557
  115.3 0.0 copy-done.5
  115.3 1.7 fusion.16
  117.1 72.1 %shard_map.95 = (f32[192,1408]{1,0:T(8,128)}, f32[88,768]{1,0:T(8,128)}) custom-call(bf16[16,192,512]{2,1,0:T(8,128)(2,1)} %bitcast.32, bf16[1408,512]{1,0:T(8,128)(2,1)} %copy-done.1, bf16[16,88,512]{2,1,0:T(8,128)(2,1)} %bitcast.28, bf16[768,512]{1,0:T(8,128)(2,1)} %get-tuple-element.12.patch_ref), custom_call_target="tpu_custom_call" | custom-call | flops 5536481280 | bytes 20000000 | tf_op jit(solution)/shard_map/pallas_call | solution.py:160
  189.2 0.0 copy-start.3
  189.2 0.0 copy-start.2
  189.2 0.0 copy-done
  189.2 1.1 copy.15
  190.3 0.0 copy-done.3
  190.3 0.7 copy.16
  191.0 0.0 copy-done.2
  191.1 1.0 copy.17
  (4 shorter events, 0.0 us)
Async XLA Ops:
  96.2 4.7 %copy-start.4 = (bf16[16,192,1408]{2,1,0:T(8,128)(2,1)S(1)}, bf16[16,192,1408]{2,1,0:T(8,128)(2,1)}, u32[]{:S(2)}) copy-start(bf16[16,192,1408]{2,1,0:T(8,128)(2,1)} %get-tuple-element.10) | copy-start | bytes 25952260
  99.8 1.1 copy-start.1
  110.4 5.0 %copy-start.5 = (bf16[3072,512]{1,0:T(8,128)(2,1)}, bf16[3072,512]{1,0:T(8,128)(2,1)S(1)}, u32[]{:S(2)}) copy-start(bf16[3072,512]{1,0:T(8,128)(2,1)S(1)} %fusion.6) | copy-start | bytes 9437188
  117.1 72.1 %copy-start = (f32[3,8,128,128]{3,2,1,0:T(8,128)S(1)}, f32[3,8,128,128]{3,2,1,0:T(8,128)}, u32[]{:S(2)}) copy-start(f32[3,8,128,128]{3,2,1,0:T(8,128)} %get-tuple-element.9) | copy-start | bytes 4718596
  189.2 1.2 copy-start.3
  189.2 1.9 copy-start.2

commit v3 on v2

--- a/solution.py
+++ b/solution.py
@@ -71,22 +71,29 @@
             )
         ]
 
+    up_width, em_width = normed_ref.shape[0], patch_ref.shape[0]
+    first_mid = (up_cut // LANES + 1) // 2 * LANES
+    other_mid = up_cut + ((up_width - up_cut) // LANES + 1) // 2 * LANES
+    up_buffers = (own_up, pair_in_up, ring_in_up, ring_out_up, up_out)
+    em_buffers = (own_em, pair_in_em, ring_in_em, ring_out_em, embed_out)
+    chunks = (
+        (0, up_buffers, slice(0, first_mid)),
+        (1, up_buffers, slice(up_cut, other_mid)),
+        (0, up_buffers, slice(first_mid, up_cut)),
+        (1, up_buffers, slice(other_mid, up_width)),
+        (0, em_buffers, slice(0, embed_cut)),
+        (1, em_buffers, slice(embed_cut, em_width)),
+    )
+
     def ring_copies(step):
-        copies = []
-        for side, neighbour in enumerate((right, left)):
-            for kind, (source, target) in enumerate(
-                ((ring_out_up, ring_in_up), (ring_out_em, ring_in_em))
-            ):
-                cut = sides[side][kind]
-                copies.append(
-                    pltpu.make_async_remote_copy(
-                        src_ref=source.at[step, :, cut], dst_ref=target.at[step, :, cut],
-                        send_sem=ring_send.at[2 * side + kind, step],
-                        recv_sem=ring_recv.at[2 * side + kind, step],
-                        device_id={"dev": neighbour}, device_id_type=MESH,
-                    )
-                )
-        return copies
+        return [
+            pltpu.make_async_remote_copy(
+                src_ref=buffers[3].at[step, :, cols], dst_ref=buffers[2].at[step, :, cols],
+                send_sem=ring_send.at[number, step], recv_sem=ring_recv.at[number, step],
+                device_id={"dev": (right, left)[side]}, device_id_type=MESH,
+            )
+            for number, (side, buffers, cols) in enumerate(chunks)
+        ]
 
     def compute(step):
         blocks = ((place + 2 * size - 1 - step) % size, (place + 1 + step) % size)
@@ -109,21 +116,19 @@
     def finish(step, first, last):
         for copy in pair_copies(step):
             copy.wait_recv()
-        up = own_up[step % 2] + pair_in_up[step].astype(jnp.float32)
-        em = own_em[step % 2] + pair_in_em[step].astype(jnp.float32)
-        if not first:
-            for copy in ring_copies(step - 1):
-                copy.wait_recv()
-            up = up + ring_in_up[step - 1].astype(jnp.float32)
-            em = em + ring_in_em[step - 1].astype(jnp.float32)
-        if last:
-            up_out[...] = up * scale
-            embed_out[...] = em * scale
-        else:
-            ring_out_up[step] = up.astype(jnp.bfloat16)
-            ring_out_em[step] = em.astype(jnp.bfloat16)
-            for copy in ring_copies(step):
-                copy.start()
+        before = None if first else ring_copies(step - 1)
+        after = None if last else ring_copies(step)
+        for number, (side, buffers, cols) in enumerate(chunks):
+            own, pair_in, ring_in, ring_out, result = buffers
+            total = own[step % 2, :, cols] + pair_in[step, :, cols].astype(jnp.float32)
+            if not first:
+                before[number].wait_recv()
+                total = total + ring_in[step - 1, :, cols].astype(jnp.float32)
+            if last:
+                result[:, cols] = total * scale
+            else:
+                ring_out[step, :, cols] = total.astype(jnp.bfloat16)
+                after[number].start()
 
     compute(0)
     compute(1)
@@ -175,8 +180,8 @@
             ],
             pltpu.SemaphoreType.DMA((2, size)),
             pltpu.SemaphoreType.DMA((2, size)),
-            pltpu.SemaphoreType.DMA((4, size)),
-            pltpu.SemaphoreType.DMA((4, size)),
+            pltpu.SemaphoreType.DMA((6, size)),
+            pltpu.SemaphoreType.DMA((6, size)),
         ],
         compiler_params=pltpu.CompilerParams(
             collective_id=0, has_side_effects=True, vmem_limit_bytes=58 * 1024 * 1024
@@ -243,25 +248,28 @@
     def index_of(spot):
         return ring_dev((spot + 2 * size) % size, size) * 2 + core
 
+    wide_end, em_end = up_ref.shape[1], em_ref.shape[1]
+
+    def pieces(step, side):
+        if step < half - 1:
+            return ((0, 0, 0, up_cut), (1, 0, up_cut, wide_end), (2, 1, 0, em_end))
+        if side == 0:
+            return ((0, 0, 0, up_cut), (2, 1, 0, em_cut))
+        return ((1, 0, up_cut, wide_end), (2, 1, em_cut, em_end))
+
     def ring_copies(step):
-        copies = []
+        copies = {}
         for side, neighbour in enumerate((right, left)):
-            spot = place - step if side == 0 else place + step
-            block = index_of(spot)
-            for kind, (mine, every, cut) in enumerate(
-                ((up_ref, up_all, up_cut), (em_ref, em_all, em_cut))
-            ):
-                source, target = mine if step == 0 else every.at[block], every.at[block]
-                if step == half - 1:
-                    cols = pl.ds(0, cut) if side == 0 else pl.ds(cut, mine.shape[1] - cut)
-                    source, target = source.at[:, cols], target.at[:, cols]
-                copies.append(
-                    pltpu.make_async_remote_copy(
-                        src_ref=source, dst_ref=target,
-                        send_sem=ring_send.at[2 * side + kind, step],
-                        recv_sem=ring_recv.at[2 * side + kind, step],
-                        device_id={"dev": neighbour}, device_id_type=MESH,
-                    )
+            block = index_of(place - step if side == 0 else place + step)
+            for chunk, kind, first, end in pieces(step, side):
+                mine, every = ((up_ref, up_all), (em_ref, em_all))[kind]
+                cols = pl.ds(first, end - first)
+                source = mine if step == 0 else every.at[block]
+                copies[chunk, side] = pltpu.make_async_remote_copy(
+                    src_ref=source.at[:, cols], dst_ref=every.at[block, :, cols],
+                    send_sem=ring_send.at[3 * side + chunk, step],
+                    recv_sem=ring_recv.at[3 * side + chunk, step],
+                    device_id={"dev": neighbour}, device_id_type=MESH,
                 )
         return copies
 
@@ -289,12 +297,14 @@
     pair_list.append((half, 2 * half - 1))
 
     def gather_step(step):
-        if step > 0:
-            for copy in ring_copies(step - 1):
-                copy.wait_recv()
-        if step < half:
-            for copy in ring_copies(step):
-                copy.start()
+        before = ring_copies(step - 1) if step > 0 else {}
+        after = ring_copies(step) if step < half else {}
+        for chunk in range(3):
+            for side in range(2):
+                if (chunk, side) in before:
+                    before[chunk, side].wait_recv()
+                if (chunk, side) in after:
+                    after[chunk, side].start()
         if step == 0:
             fresh = pair_list[:1]
         elif step < half:
@@ -410,7 +420,6 @@
     gather_step(1)
     sweep(0)
     sweep(1)
-    gather_step(2)
     sweep(2)
 
     bands = ny // PATCH_Y // size
@@ -433,7 +442,7 @@
     for offset in range(1, size):
         swap_copy(offset).start()
     income[dev] = outgo[dev]
-    for step in range(3, half):
+    for step in range(2, half):
         gather_step(step)
     for offset in range(1, size):
         swap_copy(offset).wait_recv()
@@ -481,7 +490,7 @@
     for copy in own_copies():
         copy.wait()
     for step in range(half):
-        for copy in ring_copies(step):
+        for copy in ring_copies(step).values():
             copy.wait_send()
     for shift, slot in pair_list:
         for copy in pair_copies(place + shift, slot):
@@ -526,8 +535,8 @@
             pltpu.VMEM((features, tokens), jnp.bfloat16),
             pltpu.SemaphoreType.DMA((2,)),
             pltpu.SemaphoreType.DMA((2,)),
-            pltpu.SemaphoreType.DMA((4, half)),
-            pltpu.SemaphoreType.DMA((4, half)),
+            pltpu.SemaphoreType.DMA((6, half)),
+            pltpu.SemaphoreType.DMA((6, half)),
             pltpu.SemaphoreType.DMA((2, size)),
             pltpu.SemaphoreType.DMA((2, size)),
             pltpu.SemaphoreType.DMA((2,)),

time: 192 us -> 178 us (0.927)
  Pallas kernels: 161 us -> 147 us
    pallas_call x1, Pallas kernels: 72.1 us -> 63.1 us  [scatter_grads(): pl.pallas_call(partial(scatter_kernel, size, scale, up_cut, embed_cut), o...]
    pallas_call x1, Pallas kernels: 89.1 us -> 83.9 us  [fields_and_gathers(): pl.pallas_call(partial(field_kernel, size, slab * size), out_shape=(jax.S...]
where the time goes in v3:
time: 178 us
  Pallas kernels  147 us (83%)
  matrix products  17.7 us (10%)
  local copies, waits for them, and re-layouts  7.14 us (4%)
  other arithmetic  4.65 us (3%)
    pallas_call x1, Pallas kernels, fields_and_gathers(): pl.pallas_call(partial(field_kernel, size, slab * size), out_shape=(jax.S...  83.9 us
    pallas_call x1, Pallas kernels, scatter_grads(): pl.pallas_call(partial(scatter_kernel, size, scale, up_cut, embed_cut), o...  63.1 us
    dot_general x1, matrix products, learner(): pre_act = jnp.dot(up_all, normed, preferred_element_type=jnp.float32)  9.48 us
    unnamed x16, local copies, waits for them, and re-layouts  7.14 us
    dot_general x1, matrix products, learner(): lax.dot_general(up_all, act_grad, (((0,), (0,)), ((), ())), preferred_ele...  4.95 us

profile of v3, /device:TPU:0, one launch (start us, length us, event | category | flops | bytes accessed | tf_op | source)
XLA Modules:
  0.0 177.8 jit_solution(16878499429615535250)
XLA Ops:
  1.3 1.2 broadcast_divide_fusion.inverse_ref
  2.5 1.4 multiply_reduce_fusion.strain_ref
  3.9 3.2 %copy.10 = bf16[512,3072]{0,1:T(8,128)(2,1)S(1)} copy(bf16[512,3072]{1,0:T(8,128)(2,1)} %param.13) | data formatting | bytes 6291456 | tf_op args[6]
  7.1 83.9 %shard_map.94 = (f32[3,8,128,128]{3,2,1,0:T(8,128)}, bf16[768,512]{1,0:T(8,128)(2,1)}, bf16[16,192,1408]{2,1,0:T(8,128)(2,1)}, bf16[16,88,768]{2,1,0:T(8,128)(2,1)}) custom-call(s32[8,128,128]{2,1,0:T(8,128)} %bitcast.29, f32[2,3]{1,0:T(2,128)} %broadcast_divide_fusion.inverse_ref, f32[3,3]{1,0:T(4,128)} %multiply_reduce_fusion.strain_ref, ...), custom_call_target="tpu_custom_call" | custom-call | flops 2000000000 | bytes 30000000 | tf_op jit(solution)/shard_map/pallas_call | solution.py:515
  91.0 0.0 copy-start.4
  91.0 3.2 %fusion.17 = (f32[512]{0:T(512)S(1)}, bf16[1408,512]{1,0:T(8,128)(2,1)S(1)}) fusion(bf16[1408,768]{1,0:T(8,128)(2,1)} %bitcast.33, bf16[768,512]{1,0:T(8,128)(2,1)} %get-tuple-element.12.patch_ref), kind=kOutput, calls=%fused_computation.24 | convolution fusion | flops 1110179328 | bytes 4392960 | tf_op jit(solution)/shard_map/dot_general | solution.py:559
  94.3 0.3 fusion.12.normed_ref
  94.6 0.0 copy-start.1
  94.6 1.1 copy-done.1
  95.7 0.0 copy-done.4
  95.7 9.5 %fusion.6 = bf16[3072,512]{1,0:T(8,128)(2,1)S(1)} fusion(bf16[512,3072]{0,1:T(8,128)(2,1)S(1)} %copy.10, bf16[3072,1408]{1,0:T(8,128)(2,1)S(1)} %bitcast.30, bf16[1408,512]{1,0:T(8,128)(2,1)S(1)} %fusion.12.normed_ref), kind=kOutput, calls=%fused_computation.8 | convolution fusion | flops 4462215168 | bytes 16384000 | tf_op jit(solution)/shard_map/dot_general | solution.py:564
  105.2 0.0 copy-start.5
  105.2 5.0 %fusion.13 = (f32[512]{0:T(512)S(1)}, f32[1408,512]{1,0:T(8,128)S(1)}) fusion(bf16[1408,512]{1,0:T(8,128)(2,1)S(1)} %get-tuple-element.16, f32[512]{0:T(512)S(1)} %add_rsqrt_fusion, bf16[3072,1408]{1,0:T(8,128)(2,1)S(1)} %bitcast.31, bf16[3072,512]{1,0:T(8,128)(2,1)S(1)} %fusion.6), kind=kOutput, calls=%fused_computation.20 | convolution fusion | flops 4432068096 | bytes 16125952 | tf_op jit(solution)/shard_map/dot_general | solution.py:566
  110.2 0.0 copy-done.5
  110.2 1.7 fusion.16
  111.9 63.1 %shard_map.95 = (f32[192,1408]{1,0:T(8,128)}, f32[88,768]{1,0:T(8,128)}) custom-call(bf16[16,192,512]{2,1,0:T(8,128)(2,1)} %bitcast.32, bf16[1408,512]{1,0:T(8,128)(2,1)} %copy-done.1, bf16[16,88,512]{2,1,0:T(8,128)(2,1)} %bitcast.28, bf16[768,512]{1,0:T(8,128)(2,1)} %get-tuple-element.12.patch_ref), custom_call_target="tpu_custom_call" | custom-call | flops 5536481280 | bytes 20000000 | tf_op jit(solution)/shard_map/pallas_call | solution.py:165
  175.0 0.0 copy-start.3
  175.0 0.0 copy-start.2
  175.0 0.0 copy-done
  175.0 1.1 copy.15
  176.1 0.0 copy-done.3
  176.1 0.7 copy.16
  176.8 0.0 copy-done.2
  176.9 1.0 copy.17
  (4 shorter events, 0.0 us)
Async XLA Ops:
  91.0 4.7 %copy-start.4 = (bf16[16,192,1408]{2,1,0:T(8,128)(2,1)S(1)}, bf16[16,192,1408]{2,1,0:T(8,128)(2,1)}, u32[]{:S(2)}) copy-start(bf16[16,192,1408]{2,1,0:T(8,128)(2,1)} %get-tuple-element.10) | copy-start | bytes 25952260
  94.6 1.1 copy-start.1
  105.2 5.0 %copy-start.5 = (bf16[3072,512]{1,0:T(8,128)(2,1)}, bf16[3072,512]{1,0:T(8,128)(2,1)S(1)}, u32[]{:S(2)}) copy-start(bf16[3072,512]{1,0:T(8,128)(2,1)S(1)} %fusion.6) | copy-start | bytes 9437188
  111.9 63.1 %copy-start = (f32[3,8,128,128]{3,2,1,0:T(8,128)S(1)}, f32[3,8,128,128]{3,2,1,0:T(8,128)}, u32[]{:S(2)}) copy-start(f32[3,8,128,128]{3,2,1,0:T(8,128)} %get-tuple-element.9) | copy-start | bytes 4718596
  175.0 1.2 copy-start.3
  175.0 1.9 %copy-start.2 = (f32[192,1408]{1,0:T(8,128)S(1)}, f32[192,1408]{1,0:T(8,128)}, u32[]{:S(2)}) copy-start(f32[192,1408]{1,0:T(8,128)} %get-tuple-element.24) | copy-start | bytes 3244036
